TPU v7x, 32 devices: a whole 2x2x4 slice. The times are simulated.
32 devices in a mesh: row: 8 (over y, x, core), col: 4 (over z).
Axes of the slice: x: 2, y: 2, z: 4, core: 2. Of those that a mesh axis runs over, the one named last changes fastest.
Arguments:
- single: float32 [512, 768], P('row', 'col'), may hold values from -6 to 6
- pair: float32 [512, 512, 128], P('row', 'col'), may hold values from -6 to 6
- single_gain: float32 [768], replicated, may hold values from 0.25 to 1.75
- pair_gain: float32 [128], replicated, may hold values from 0.25 to 1.75
- w_query: float32 [768, 768], replicated, may hold values from -0.25 to 0.25
- w_key: float32 [768, 768], replicated, may hold values from -0.25 to 0.25
- w_value: float32 [768, 768], replicated, may hold values from -0.21875 to 0.21875
- w_gate: float32 [768, 768], replicated, may hold values from -0.21875 to 0.21875
- w_bias: float32 [128, 16], replicated, may hold values from -0.5 to 0.5
- w_out: float32 [768, 768], P(None, 'col'), may hold values from -0.21875 to 0.21875
- cotangent: float32 [512, 768], P('row', 'col'), may hold values from -6 to 6
Outputs:
- attended: float32 [512, 768], P('row', 'col')
- pair_grad: float32 [512, 512, 128], P('row', 'col')
- bias_grad: float32 [128, 16], replicated
All inputs are finite; a program needn't handle non-finite values.
Results may differ from a plain program's by a relative error of at most 0.0003.
Values sent between devices are 32-bit elements; how exact they have to be, the bound alone decides.
A program may use at most 128 MiB of HBM per device.

v0:
```python
import jax
import jax.numpy as jnp
from jax import lax
from jax.sharding import PartitionSpec as P


def joined(array, axis, combine):
    everything = jax.tree.map(lambda part: lax.all_gather(part, axis), array)
    initial = jax.tree.map(lambda part: part[0], everything)

    def lap(k, so_far):
        return combine(so_far, jax.tree.map(lambda part: part[k], everything))

    return lax.fori_loop(1, lax.axis_size(axis), lap, initial)


def layer_norm(values_in, gain):
    centre = jnp.mean(values_in, axis=-1, keepdims=True)
    spread = jnp.mean((values_in - centre) ** 2, axis=-1, keepdims=True)
    return (values_in - centre) * lax.rsqrt(spread + 1e-05) * gain


def combine_parts(earlier, later):
    max_a, total_a, acc_a = earlier
    max_b, total_b, acc_b = later
    top_max = jnp.maximum(max_a, max_b)
    factor_a = jnp.exp(max_a - top_max)
    factor_b = jnp.exp(max_b - top_max)
    return (
        top_max,
        total_a * factor_a + total_b * factor_b,
        acc_a * factor_a[:, :, None] + acc_b * factor_b[:, :, None],
    )


def local(
    single, pair, single_gain, pair_gain, w_query, w_key, w_value, w_gate, w_bias, w_out, cotangent
):
    highest = lax.Precision.HIGHEST
    width_model = single_gain.shape[0]
    head_count = w_bias.shape[1]
    head_dim = width_model // head_count
    query_count = pair.shape[0]
    key_count = pair.shape[1]
    row_tokens = lax.all_gather(single, "col", axis=1, tiled=True)
    normed = layer_norm(row_tokens, single_gain)
    query = jnp.dot(normed, w_query, precision=highest).reshape(query_count, head_count, head_dim)
    gating = jax.nn.sigmoid(jnp.dot(normed, w_gate, precision=highest))
    col_index = lax.axis_index("col")
    kv_rows = jnp.concatenate(
        [jnp.dot(normed, w_key, precision=highest), jnp.dot(normed, w_value, precision=highest)],
        axis=1,
    )
    all_kv = lax.all_gather(kv_rows, "row", axis=0, tiled=True)
    key_source = lax.dynamic_slice_in_dim(all_kv, col_index * key_count, key_count, 0)
    keys = key_source[:, :width_model].reshape(key_count, head_count, head_dim)
    values = key_source[:, width_model:].reshape(key_count, head_count, head_dim)

    def bias_of(pair_tile, weight):
        return jnp.einsum(
            "ijc,ch->ihj", layer_norm(pair_tile, pair_gain), weight, precision=highest
        )

    bias, pull = jax.vjp(bias_of, pair, w_bias)
    scores = jnp.einsum("ihd,jhd->ihj", query, keys, precision=highest) * head_dim ** (-0.5) + bias
    local_max = jnp.max(scores, axis=-1)
    expo = jnp.exp(scores - local_max[:, :, None])
    local_total = jnp.sum(expo, axis=-1)
    local_acc = jnp.einsum("ihj,jhd->ihd", expo, values, precision=highest)
    top_max, top_total, top_acc = joined((local_max, local_total, local_acc), "col", combine_parts)
    context = top_acc / top_total[:, :, None]
    attended = jnp.dot(gating * context.reshape(query_count, width_model), w_out, precision=highest)
    back_sum = lax.psum(jnp.dot(cotangent, w_out.T, precision=highest), "col")
    d_context = (back_sum * gating).reshape(query_count, head_count, head_dim)
    row_delta = jnp.sum(d_context * context, axis=-1)
    soft_weights = jnp.exp(scores - top_max[:, :, None]) / top_total[:, :, None]
    d_probs = jnp.einsum("ihd,jhd->ihj", d_context, values, precision=highest)
    d_scores = soft_weights * (d_probs - row_delta[:, :, None])
    pair_grad, weight_part = pull(d_scores)
    bias_grad = lax.psum(weight_part, ("row", "col"))
    return (attended, pair_grad, bias_grad)


def solution(mesh):
    placed = (
        P("row", "col"),
        P("row", "col", None),
        P(),
        P(),
        P(),
        P(),
        P(),
        P(),
        P(),
        P(None, "col"),
        P("row", "col"),
    )
    return jax.shard_map(
        local,
        mesh=mesh,
        in_specs=placed,
        out_specs=(P("row", "col"), P("row", "col", None), P()),
        check_vma=False,
    )
```

profile of v0, /device:TPU:0, one launch (start us, length us, event | category | flops | bytes accessed | tf_op | source)
XLA Modules:
  0.0 231.6 jit_solution(13436417849575303428)
XLA Ops:
  8.1 2.4 %fusion.39 = f32[64,768]{1,0:T(8,128)} fusion(f32[64,192]{1,0:T(8,128)} %param.23, f32[768,192]{0,1:T(8,128)} %param.22), kind=kOutput, calls=%fused_computation.70 | convolution fusion | flops 113246208 | bytes 835584 | tf_op jit(solution)/shard_map/dot_general | solution.py:73
  10.5 16.5 %all-gather.3 = f32[4,192,64]{1,2,0:T(8,128)S(1)} all-gather(f32[1,192,64]{1,2,0:T(8,128)} %bitcast.97), channel_id=1, replica_groups=mesh['row'=8,'col'=4] {'col'}, dimensions={0}, use_global_device_ids=true | all-gather | bytes 245760 | tf_op jit(solution)/shard_map/all_gather | solution.py:45
  27.1 0.2 copy.52
  27.2 0.1 reduce_sum.89
  27.4 0.2 reshape.83
  27.6 0.2 multiply_reduce_fusion.5
  27.8 3.4 %fusion.34 = f32[64,768]{1,0:T(8,128)S(1)} fusion(f32[768,768]{1,0:T(8,128)} %param.18, f32[768,64]{0,1:T(8,128)S(1)} %reshape.83, f32[768]{0:T(1024)} %param.15, f32[64]{0:T(128)S(1)} %add_rsqrt_fusion, f32[64]{0:T(128)S(1)} %broadcast_multiply_fusion.1), kind=kOutput, calls=%fused_computation.66 | convolution fusion | flops 453132288 | bytes 2756096 | tf_op jit(solution)/shard_map/dot_general | solution.py:51
  31.2 1.6 fusion.33
  32.7 0.8 pad_maximum_fusion
  33.5 3.3 %reduce_sum.91 = f32[64,128]{1,0:T(8,128)S(1)} reduce(f32[64,128,128]{2,1,0:T(8,128)} %param.14, f32[]{:T(128)} %constant.60.clone.1), dimensions={2}, to_apply=%region_2.0 | reduce | flops 1040384 | bytes 4227076 | tf_op jit(solution)/shard_map/jvp()/reduce_sum | solution.py:18
  36.9 5.8 %copy.55 = f32[64,128,128]{1,2,0:T(8,128)} copy(f32[64,128,128]{2,1,0:T(8,128)} %param.14) | data formatting | bytes 8388608 | tf_op args[1]
  42.7 3.2 %multiply_reduce_fusion.1 = f32[64,128]{1,0:T(8,128)S(1)} fusion(f32[64,128,128]{1,2,0:T(8,128)} %copy.55, f32[64,128]{1,0:T(8,128)S(1)} %broadcast_multiply_fusion), kind=kLoop, calls=%fused_computation.11 | loop fusion | flops 3137536 | bytes 4259840 | tf_op jit(solution)/shard_map/jvp()/reduce_sum | solution.py:19
  46.0 6.3 %fusion.35 = f32[64,768]{0,1:T(8,128)} fusion(f32[768,768]{1,0:T(8,128)} %param.17, f32[768,64]{0,1:T(8,128)S(1)} %reshape.83, f32[768]{0:T(1024)S(1)} %copy-done.13, f32[64]{0:T(128)S(1)} %add_rsqrt_fusion, f32[64]{0:T(128)S(1)} %broadcast_multiply_fusion.1), kind=kOutput, calls=%fused_computation.67 | convolution fusion | flops 453132288 | bytes 2756096 | tf_op jit(solution)/shard_map/reshape | solution.py:47
  52.2 2.7 %fusion.4 = f32[64,128,16]{1,2,0:T(8,128)S(1)} fusion(f32[64,128,128]{1,2,0:T(8,128)S(1)} %copy-done.1, f32[128]{0:T(128)S(1)} %copy-done.16, f32[64,128]{1,0:T(8,128)S(1)} %fusion.29, f32[64,128]{1,0:T(8,128)S(1)} %broadcast_multiply_fusion, f32[128,16]{0,1:T(8,128)S(1)} %copy-done.14), kind=kOutput, calls=%fused_computation.15 | convolution fusion | flops 204472320 | bytes 4792832 | tf_op jit(solution)/shard_map/jvp(ijc,ch->ihj)/dot_general | solution.py:60
  55.0 3.3 %fusion.38 = (f32[64,768]{1,0:T(8,128)S(1)}, f32[64,768]{1,0:T(8,128)}) fusion(f32[64,768]{1,0:T(8,128)} %all-reduce.2.cloned.1.call-done, f32[768,768]{1,0:T(8,128)S(1)} %copy-done, f32[768,64]{0,1:T(8,128)S(1)} %reshape.83, f32[768]{0:T(1024)S(1)} %copy-done.13, f32[64]{0:T(128)S(1)} %add_rsqrt_fusion, f32[64]{0:T(128)S(1)} %broadcast_multiply_fusion.1), kind=kOutput, calls=%fused_computation.69 | convolution fusion | flops 453328896 | bytes 3149312 | tf_op jit(solution)/shard_map/dot_general | solution.py:48
  58.3 1.1 reshape.72
  59.3 8.1 %all-gather.8.cloned.1.call-done = f32[512,1536]{1,0:T(8,128)} async-done(((f32[64,1536]{1,0:T(8,128)}), f32[512,1536]{1,0:T(8,128)}) %all-gather.8.cloned.1.call-update) | async-done | bytes 3145744 | tf_op jit(solution)/shard_map/all_gather | solution.py:54
  67.4 2.1 fusion.37
  69.5 1.1 copy.58
  70.7 2.0 copy.53
  72.7 2.3 %fusion.32 = (f32[64,16]{0,1:T(8,128)S(1)}, f32[16,128,64]{1,2,0:T(8,128)S(1)}) fusion(f32[64,128,16]{1,2,0:T(8,128)S(1)} %fusion.4, f32[128,16,48]{0,2,1:T(8,128)} %bitcast.92, f32[64,16,48]{0,2,1:T(8,128)} %bitcast.93), kind=kOutput, calls=%fused_computation.64 | convolution fusion | flops 75889664 | bytes 1642496 | tf_op jit(solution)/shard_map/ihd,jhd->ihj/dot_general | solution.py:65
  75.1 0.4 fusion.25
  75.5 13.9 %all-gather.5 = f32[4,64,16]{1,2,0:T(8,128)} all-gather(f32[1,64,16]{1,2,0:T(8,128)S(1)} %bitcast.98), channel_id=3, replica_groups=mesh['row'=8,'col'=4] {'col'}, dimensions={0}, use_global_device_ids=true | all-gather | bytes 20480 | tf_op jit(solution)/shard_map/all_gather | solution.py:8
  89.3 0.7 slice_bitcast_fusion
  90.0 14.0 %all-gather.4 = f32[4,64,16]{1,2,0:T(8,128)} all-gather(f32[1,64,16]{1,2,0:T(8,128)S(1)} %bitcast.95), channel_id=2, replica_groups=mesh['row'=8,'col'=4] {'col'}, dimensions={0}, use_global_device_ids=true | all-gather | bytes 20480 | tf_op jit(solution)/shard_map/all_gather | solution.py:8
  104.0 1.3 slice_bitcast_fusion.1
  105.3 1.8 convolution_bitcast_fusion
  107.2 1.3 copy.59
  108.5 33.4 %all-gather.2 = f32[256,16,48]{2,1,0:T(8,128)S(1)} all-gather(f32[64,16,48]{2,1,0:T(8,128)S(1)} %copy.59), channel_id=4, replica_groups=mesh['row'=8,'col'=4] {'col'}, dimensions={0}, use_global_device_ids=true | all-gather | bytes 983040 | tf_op jit(solution)/shard_map/all_gather | solution.py:8
  141.9 1.3 copy-done.4
  143.3 8.9 %while.19 = (s32[]{:T(128)}, f32[64,16]{0,1:T(8,128)}, f32[64,16]{0,1:T(8,128)S(1)}, f32[64,16,48]{2,1,0:T(8,128)S(1)}, f32[4,64,16]{1,2,0:T(8,128)}, /*index=5*...) while((s32[]{:T(128)}, f32[64,16]{0,1:T(8,128)}, ...), condition=%wide.region_7.0_spmd, body=%wide.region_6.0_spmd.sunk | while | flops 153605 | bytes 647311 | solution.py:14
  143.3 1.3 fusion.53
  144.8 1.4 fusion.54
  146.2 1.3 fusion.53
  147.7 1.4 fusion.54
  149.2 1.3 fusion.53
  150.7 1.4 fusion.54
  152.1 0.1 copy.60
  152.2 2.0 multiply_reduce_fusion.4
  154.3 2.4 %fusion.13 = f32[16,64,128]{2,1,0:T(8,128)S(1)} fusion(f32[128,16,48]{0,2,1:T(8,128)} %bitcast.91, f32[16,128,64]{1,2,0:T(8,128)} %copy-done.5, f32[64,16,48]{2,1,0:T(8,128)} %reshape.72, f32[64,128,16]{1,2,0:T(8,128)S(1)} %fusion.4, f32[16,64]{1,0:T(8,128)S(1)} %copy.63, f32[16,64]{1,0:T(8,128)S(1)} %bitcast.94, f32[16,64]{1,0:T(8,128)} %bitcast.19), kind=kOutput, calls=%fused_computation.25 | convolution fusion | flops 76152832 | bytes 2174976 | tf_op jit(solution)/shard_map/ihd,jhd->ihj/dot_general | solution.py:77
  156.8 5.7 %fusion.17 = f32[128,16]{0,1:T(8,128)S(1)} fusion(f32[64,128,128]{1,2,0:T(8,128)} %copy.55, f32[128]{0:T(128)} %param.16, f32[64,128]{1,0:T(8,128)S(1)} %fusion.29, f32[64,128]{1,0:T(8,128)S(1)} %broadcast_multiply_fusion, f32[16,64,128]{2,1,0:T(8,128)S(1)} %fusion.13), kind=kOutput, calls=%fused_computation.32 | convolution fusion | flops 204472320 | bytes 4792832 | tf_op jit(solution)/shard_map/transpose(jvp(ijc,ch->ihj))/dot_general | solution.py:60
  162.5 6.7 %multiply_reduce_fusion.3 = (f32[64,128]{1,0:T(8,128)S(1)}, f32[64,128]{1,0:T(8,128)S(1)}, f32[64,128,128]{1,2,0:T(8,128)}) fusion(f32[128]{0:T(128)} %param.16, f32[64,128]{1,0:T(8,128)S(1)} %fusion.29, f32[64,128,128]{1,2,0:T(8,128)S(1)} %copy-done.2, f32[64,128]{1,0:T(8,128)S(1)} %broadcast_multiply_fusion, f32[128,16]{0,1:T(8,128)S(1)} %copy-done.15, ...), kind=kOutput, calls=%fused_computation.13 | convolution fusion | flops 207601664 | bytes 9052672 | tf_op jit(solution)/shard_map/transpose(jvp(ijc,ch->ihj))/dot_general | solution.py:60
  169.2 38.6 %psum.15 = f32[128,16]{0,1:T(8,128)} all-reduce(f32[128,16]{0,1:T(8,128)S(1)} %fusion.17), channel_id=1, replica_groups=mesh['row'=8,'col'=4] {'row','col'}, use_global_device_ids=true, to_apply=%region_13.0 | all-reduce | flops 2048 | bytes 16384 | tf_op jit(solution)/shard_map/psum | solution.py:80
  207.8 0.2 reshape.71
  208.1 3.4 %multiply_reduce_fusion.2 = f32[64,128]{1,0:T(8,128)S(1)} fusion(f32[64,128,128]{1,2,0:T(8,128)} %copy.55, f32[64,128]{1,0:T(8,128)S(1)} %multiply_multiply_fusion.6, f32[64,128]{1,0:T(8,128)S(1)} %broadcast_multiply_fusion), kind=kLoop, calls=%fused_computation.12 | loop fusion | flops 3137536 | bytes 4292608 | tf_op jit(solution)/shard_map/transpose(jvp())/reduce_sum | solution.py:19
  211.6 5.6 %add_add_fusion = f32[64,128,128]{1,2,0:T(8,128)} fusion(f32[64,128,128]{1,2,0:T(8,128)} %get-tuple-element.235, f32[64,128,128]{1,2,0:T(8,128)S(1)} %copy-done.3, f32[64,128]{1,0:T(8,128)S(1)} %add_multiply_fusion, f32[64,128]{1,0:T(8,128)S(1)} %multiply_multiply_fusion.6, f32[128]{0:T(128)S(1)} %copy-done.17, f32[64,128]{1,0:T(8,128)S(1)} %fusion.29, ...), kind=kLoop, calls=%fused_computation.8 | loop fusion | flops 6291456 | bytes 12714496 | tf_op jit(solution)/shard_map/transpose(jvp())/add_any | solution.py:18
  217.2 5.7 %copy.67 = f32[64,128,128]{2,1,0:T(8,128)} copy(f32[64,128,128]{1,2,0:T(8,128)} %add_add_fusion) | data formatting | bytes 8388608
  222.9 1.3 fusion.27
  (54 shorter events, 0.9 us)
Async XLA Ops:
  8.0 47.0 %copy-start = (f32[768,768]{1,0:T(8,128)S(1)}, f32[768,768]{1,0:T(8,128)}, u32[]{:S(2)}) copy-start(f32[768,768]{1,0:T(8,128)} %param.20) | copy-start | bytes 7077892
  8.0 23.1 %copy-start.13 = (f32[768]{0:T(1024)S(1)}, f32[768]{0:T(1024)}, u32[]{:S(2)}) copy-start(f32[768]{0:T(1024)} %param.15) | copy-start | bytes 9220
  8.0 47.0 %all-reduce.2.cloned.1.call-start = ((), (), s32[]{:S(2)}) async-start(), calls=%async_computation.1 | async-start | bytes 393216 | tf_op jit(solution)/shard_map/psum | solution.py:73
  10.5 57.0 %all-gather.8.cloned.1.call-start = ((), (), s32[]{:S(2)}) async-start(), calls=%async_computation | async-start | bytes 3538944 | tf_op jit(solution)/shard_map/all_gather | solution.py:54
  27.5 3.6 %copy-start.6 = (f32[768,768]{1,0:T(8,128)S(1)}, f32[768,768]{1,0:T(8,128)}, u32[]{:S(2)}) copy-start(f32[768,768]{1,0:T(8,128)} %param.19) | copy-start | bytes 7077892
  42.7 9.6 %copy-start.14 = (f32[128,16]{0,1:T(8,128)S(1)}, f32[128,16]{0,1:T(8,128)}, u32[]{:S(2)}) copy-start(f32[128,16]{0,1:T(8,128)} %param.21) | copy-start | bytes 24580
  42.7 9.6 %copy-start.16 = (f32[128]{0:T(128)S(1)}, f32[128]{0:T(128)}, u32[]{:S(2)}) copy-start(f32[128]{0:T(128)} %param.16) | copy-start | bytes 1540
  42.7 9.6 %copy-start.1 = (f32[64,128,128]{1,2,0:T(8,128)S(1)}, f32[64,128,128]{1,2,0:T(8,128)}, u32[]{:S(2)}) copy-start(f32[64,128,128]{1,2,0:T(8,128)} %copy.55) | copy-start | bytes 12582916
  45.9 9.0 %copy-start.11 = (f32[64,128]{1,0:T(8,128)}, f32[64,128]{1,0:T(8,128)S(1)}, u32[]{:S(2)}) copy-start(f32[64,128]{1,0:T(8,128)S(1)} %multiply_reduce_fusion.1) | copy-start | bytes 98308
  70.7 34.7 %copy-start.9 = (f32[128,768]{0,1:T(8,128)}, f32[128,768]{0,1:T(8,128)S(1)}, u32[]{:S(2)}) copy-start(f32[128,768]{0,1:T(8,128)S(1)} %copy.58) | copy-start | bytes 1179652
  75.0 30.3 %copy-start.5 = (f32[16,128,64]{1,2,0:T(8,128)}, f32[16,128,64]{1,2,0:T(8,128)S(1)}, u32[]{:S(2)}) copy-start(f32[16,128,64]{1,2,0:T(8,128)S(1)} %get-tuple-element.234) | copy-start | bytes 1572868
  141.9 1.4 copy-start.4
  154.3 8.2 %copy-start.15 = (f32[128,16]{0,1:T(8,128)S(1)}, f32[128,16]{0,1:T(8,128)}, u32[]{:S(2)}) copy-start(f32[128,16]{0,1:T(8,128)} %param.21) | copy-start | bytes 24580
  154.3 8.2 %copy-start.2 = (f32[64,128,128]{1,2,0:T(8,128)S(1)}, f32[64,128,128]{1,2,0:T(8,128)}, u32[]{:S(2)}) copy-start(f32[64,128,128]{1,2,0:T(8,128)} %copy.55) | copy-start | bytes 12582916
  162.5 45.3 %copy-start.8 = (f32[64,16,48]{2,1,0:T(8,128)S(1)}, f32[64,16,48]{2,1,0:T(8,128)}, u32[]{:S(2)}) copy-start(f32[64,16,48]{2,1,0:T(8,128)} %get-tuple-element.228) | copy-start | bytes 589828
  162.5 45.6 %copy-start.12 = (f32[64,128]{1,0:T(8,128)S(1)}, f32[64,128]{1,0:T(8,128)}, u32[]{:S(2)}) copy-start(f32[64,128]{1,0:T(8,128)} %copy-done.11) | copy-start | bytes 98308
  169.2 42.3 %copy-start.17 = (f32[128]{0:T(128)S(1)}, f32[128]{0:T(128)}, u32[]{:S(2)}) copy-start(f32[128]{0:T(128)} %param.16) | copy-start | bytes 1540
  208.1 3.5 %copy-start.3 = (f32[64,128,128]{1,2,0:T(8,128)S(1)}, f32[64,128,128]{1,2,0:T(8,128)}, u32[]{:S(2)}) copy-start(f32[64,128,128]{1,2,0:T(8,128)} %copy.55) | copy-start | bytes 12582916
  217.2 5.7 %copy-start.7 = (f32[768,192]{0,1:T(8,128)S(1)}, f32[768,192]{0,1:T(8,128)}, u32[]{:S(2)}) copy-start(f32[768,192]{0,1:T(8,128)} %param.22) | copy-start | bytes 1769476
  217.2 5.7 %copy-start.10 = (f32[64,768]{1,0:T(8,128)S(1)}, f32[64,768]{1,0:T(8,128)}, u32[]{:S(2)}) copy-start(f32[64,768]{1,0:T(8,128)} %get-tuple-element.232) | copy-start | bytes 589828
Sparse Core Ops, SparseCore 0:
  11.2 38.5 all-reduce.1
Sparse Core Ops, SparseCore 1:
  33.6 33.8 all-gather.7
where the time goes:
time: 233 us; the launch traced here: 232 us
  blocking collectives  116 us (50%)
  matrix products  39.9 us (17%)
  other arithmetic  27.5 us (12%)
  local copies, waits for them, and re-layouts  23.7 us (10%)
  between operations  15.7 us (7%)
  waiting for transfers between devices  8.17 us (4%)
    all_gather x3, blocking collectives, joined(): everything = jax.tree.map(lambda part: lax.all_gather(part, axis), array)  61.3 us
    psum x1, blocking collectives, local(): bias_grad = lax.psum(weight_part, ('row', 'col'))  38.6 us
    all_gather x1, blocking collectives, local(): row_tokens = lax.all_gather(single, 'col', axis=1, tiled=True)  16.5 us
    dot_general x3, matrix products, bias_of(): jnp.einsum('ijc,ch->ihj', layer_norm(pair_tile, pair_gain), weight, preci...  15.1 us
    unnamed x39, local copies, waits for them, and re-layouts  13 us
    all_gather x1, waiting for transfers between devices, local(): all_kv = lax.all_gather(kv_rows, 'row', axis=0, tiled=True)  8.12 us
    reduce_sum x3, other arithmetic, layer_norm(): spread = jnp.mean((values_in - centre) ** 2, axis=-1, keepdims=True)  6.86 us
    reshape x1, matrix products, local(): jnp.dot(normed, w_query, precision=highest)  6.28 us
  transfers between devices with their start and end apart: 2, of which 1 were waited for; matrix products, arithmetic and copies ran while one was open for 14% of the time, Pallas kernels for 0%

commit v1 on v0

v1 whole, which is shorter than its diff:
```python
import functools

import jax
import jax.numpy as jnp
from jax import lax
from jax.experimental import pallas as pl
from jax.experimental.pallas import tpu as pltpu
from jax.sharding import PartitionSpec as P

MESH = pl.DeviceIdType.MESH
VMEM_LIMIT = 56 * 1024 * 1024
CHUNK = 8
F32 = jnp.float32
BF16 = jnp.bfloat16
NN = (((1,), (0,)), ((), ()))
NT = (((1,), (1,)), ((), ()))


def split(x):
    hi = x.astype(BF16)
    return hi, (x - hi.astype(F32)).astype(BF16)


def stacked(x):
    return jnp.concatenate(split(x), axis=0)


def dot(a, b, dims):
    return lax.dot_general(a, b, dims, preferred_element_type=F32)


def dot3(both, b_hi, b_lo, dims):
    m = both.shape[0] // 2
    high = dot(both, b_hi, dims)
    return high[:m] + high[m:] + dot(both[:m], b_lo, dims)


def unit(x, width):
    centre = jnp.sum(x, axis=-1, keepdims=True) * (1.0 / width)
    x = x - centre
    spread = jnp.sum(x * x, axis=-1, keepdims=True) * (1.0 / width)
    scale = lax.rsqrt(spread + 1e-05)
    return x * scale, scale


def remote(src, dst, send_sem, recv_sem, **device):
    return pltpu.make_async_remote_copy(
        src_ref=src, dst_ref=dst, send_sem=send_sem, recv_sem=recv_sem,
        device_id=device, device_id_type=MESH,
    )


def greet(devices):
    barrier = pltpu.get_barrier_semaphore()
    for device in devices:
        pl.semaphore_signal(barrier, inc=1, device_id=device, device_id_type=MESH)
    pl.semaphore_wait(barrier, len(devices))


def scores_kernel(
    n_row, n_col, heads,
    single_ref, pair_hbm, gain_ref, pgain_ref, wq_hbm, wk_hbm, wv_hbm, wg_hbm, wbt_ref, wout_ref,
    cot_ref,
    att_ref, ds_ref,
    pair_v, wq_v, wk_v, wv_v, wg_v,
    tok, keyb, part_out, part_in, back, s_ref, dp_ref, q_ref, dc_ref, gate_b,
    kb_hi, kb_lo, vb_hi, vb_lo, stat, ctx_ref, ctx_out, ctx_in, gctx,
    w_sem, p_sem, send_sem, recv_sem, tree_send, tree_recv, mate_send, mate_recv,
):
    r = lax.axis_index("row")
    c = lax.axis_index("col")
    tq, blk = single_ref.shape
    width = blk * n_col
    dim = width // heads
    n_chunk = tq // CHUNK
    n_chip = n_row // 2
    bits = n_chip.bit_length() - 1
    parity = r % 2
    chip = r // 2

    weights = [(wq_hbm, wq_v), (wg_hbm, wg_v), (wk_hbm, wk_v), (wv_hbm, wv_v)]
    pair_copies = [
        pltpu.make_async_copy(
            pair_hbm.at[pl.ds(CHUNK * k, CHUNK)], pair_v.at[pl.ds(CHUNK * k, CHUNK)], p_sem.at[k]
        )
        for k in range(n_chunk)
    ]
    weight_copies = [
        pltpu.make_async_copy(src, dst, w_sem.at[k]) for k, (src, dst) in enumerate(weights)
    ]
    for copy in pair_copies[:2] + weight_copies + pair_copies[2:]:
        copy.start()

    def peer(d):
        return (c + d) % n_col

    mate = r + 1 - 2 * parity
    chip_bits = [(chip // (1 << e)) % 2 for e in range(bits)]
    col_bits = [(c // (1 << e)) % 2 for e in range(bits)]
    away = [a + b - 2 * a * b for a, b in zip(chip_bits, col_bits)]
    beside = [r + (2 << e) * (1 - 2 * chip_bits[e]) for e in range(bits)]
    greet(
        [{"col": peer(d)} for d in range(1, n_col)]
        + [{"row": row} for row in beside]
        + [{"row": mate}]
    )

    def spread_out(stage, src_of, dst_of):
        copies = []
        for d in range(1, n_col):
            copy = remote(
                src_of(d), dst_of(d), send_sem.at[stage, d], recv_sem.at[stage, d], col=peer(d)
            )
            copy.start()
            copies.append(copy)
        return copies

    tok_copies = spread_out(0, lambda d: single_ref, lambda d: tok.at[c])
    tok[c] = single_ref[...]

    cot = stacked(cot_ref[...])

    def part(owner):
        rows = wout_ref[pl.ds(pl.multiple_of(owner * blk, 8), blk), :]
        return dot3(cot, *split(rows), NT)

    for d in range(1, n_col):
        part_out[d] = part(peer(d))
    back_copies = spread_out(1, lambda d: part_out.at[d], lambda d: part_in.at[d])
    part_out[0] = part(c)

    wb = stacked(wbt_ref[...] * pgain_ref[...])

    def pair_bias(k):
        pair_copies[k].wait()
        x = pair_v[pl.ds(CHUNK * k, CHUNK)]
        x, _ = unit(x, x.shape[-1])
        hi, lo = split(x.reshape(-1, x.shape[-1]))
        bias = dot(wb, hi, NT)
        bias = bias[:heads] + bias[heads:] + dot(wb[:heads], lo, NT)
        keys_here = s_ref.shape[2]
        for i in range(CHUNK):
            s_ref[CHUNK * k + i] = bias[:, i * keys_here : (i + 1) * keys_here]

    at_source = sum(away) == 0
    forwards = []
    for t in range(n_col):
        block = (c - t + n_col) % n_col
        if t:
            tok_copies[t - 1].wait_recv()

        @pl.when(at_source)
        def _():
            keyb[parity, block] = tok[block]

        @pl.when(jnp.logical_not(at_source))
        def _():
            remote(
                keyb.at[parity, block], keyb.at[parity, block], tree_send.at[0, t],
                tree_recv.at[t], row=mate,
            ).wait_recv()

        for e in reversed(range(bits)):
            copy = remote(
                keyb.at[parity, block], keyb.at[parity, block], tree_send.at[e, t],
                tree_recv.at[t], row=beside[e],
            )
            forwards.append((sum(away[: e + 1]) == 0, copy))
            pl.when(forwards[-1][0])(copy.start)
        copy = remote(
            keyb.at[parity, block], keyb.at[parity, block], mate_send.at[t], mate_recv.at[t],
            row=mate,
        )
        copy.start()
        forwards.append((None, copy))
        for k in range(t * n_chunk // n_col, (t + 1) * n_chunk // n_col):
            pair_bias(k)

    for copy in back_copies:
        copy.wait_recv()
    total = part_out[0]
    for d in range(1, n_col):
        total = total + part_in[d]
    back[c] = total
    back_copies2 = spread_out(2, lambda d: back.at[c], lambda d: back.at[c])

    def project(both, w_ref):
        step = 256
        out = None
        for lo in range(0, width, step):
            piece = dot3(both[:, lo : lo + step], *split(w_ref[lo : lo + step, :]), NN)
            out = piece if out is None else out + piece
        return out

    def joined(ref, *lead):
        return jnp.concatenate([ref[(*lead, b)] for b in range(n_col)], axis=1)

    rows = stacked(unit(joined(tok), width)[0] * gain_ref[...])
    weight_copies[0].wait()
    q_ref[...] = project(rows, wq_v) * dim ** (-0.5)
    weight_copies[1].wait()
    gate = jax.nn.sigmoid(project(rows, wg_v))
    for b in range(n_col):
        gate_b[b] = gate[:, b * blk : (b + 1) * blk]

    for _, copy in forwards[bits :: bits + 1]:
        copy.wait_recv()
    tokens = jnp.concatenate([joined(keyb, 0), joined(keyb, 1)], axis=0)
    rows = stacked(unit(tokens, width)[0] * gain_ref[...])
    weight_copies[2].wait()
    kb_hi[...], kb_lo[...] = split(project(rows, wk_v))
    weight_copies[3].wait()
    vb_hi[...], vb_lo[...] = split(project(rows, wv_v))

    for copy in back_copies2:
        copy.wait_recv()
    dc_ref[...] = joined(back) * gate

    head_of = lax.broadcasted_iota(jnp.int32, (heads, width), 0) * dim
    feature = lax.broadcasted_iota(jnp.int32, (heads, width), 1)
    mask = jnp.where((feature >= head_of) & (feature < head_of + dim), 1.0, 0.0)
    flat = CHUNK * heads

    def by_head(ref, k):
        x = ref[pl.ds(pl.multiple_of(CHUNK * k, CHUNK), CHUNK), :]
        return stacked((x[:, None, :] * mask[None]).reshape(flat, width))

    lane = lax.broadcasted_iota(jnp.int32, (flat, 128), 1)

    def forward(k, carry):
        here = pl.ds(CHUNK * k, CHUNK)
        s = s_ref[here].reshape(flat, -1)
        s = s + dot3(by_head(q_ref, k), kb_hi[...], kb_lo[...], NT)
        top = jnp.max(s, axis=-1, keepdims=True)
        expo = jnp.exp(s - top)
        dp = dot3(by_head(dc_ref, k), vb_hi[...], vb_lo[...], NT)
        sums = jnp.sum(expo, axis=-1, keepdims=True)
        delta = jnp.sum(expo * dp, axis=-1, keepdims=True)
        s_ref[here] = expo.reshape(CHUNK, heads, -1)
        dp_ref[here] = dp.reshape(CHUNK, heads, -1)
        packed = jnp.where(lane == 0, top, jnp.where(lane == 1, sums, delta))
        stat[c, k] = packed.T[:8]
        return carry

    lax.fori_loop(0, n_chunk, forward, 0)
    stat_copies = spread_out(3, lambda d: stat.at[c], lambda d: stat.at[c])
    for copy in stat_copies:
        copy.wait_recv()

    def backward(k, carry):
        here = pl.ds(CHUNK * k, CHUNK)
        every = [stat[b, k] for b in range(n_col)]
        top = functools.reduce(jnp.maximum, [x[0:1] for x in every])
        factors = [jnp.exp(x[0:1] - top) for x in every]
        sums = sum(f * x[1:2] for f, x in zip(factors, every))
        delta = sum(f * x[2:3] for f, x in zip(factors, every)) / sums
        mine = jnp.exp(stat[c, k][0:1] - top) / sums
        sub = lax.broadcasted_iota(jnp.int32, (128, flat), 0)
        columns = jnp.where(sub == 0, mine, delta).T
        probs = s_ref[here].reshape(flat, -1) * columns[:, 0:1]
        ds = probs * (dp_ref[here].reshape(flat, -1) - columns[:, 1:2])
        ds_ref[here] = ds.reshape(CHUNK, heads, -1)
        wide = dot3(stacked(probs), vb_hi[...], vb_lo[...], NN).reshape(CHUNK, heads, width)
        ctx_ref[pl.ds(pl.multiple_of(CHUNK * k, CHUNK), CHUNK), :] = jnp.sum(wide * mask[None], axis=1)
        return carry

    lax.fori_loop(0, n_chunk, backward, 0)
    ctx = ctx_ref[...]
    for b in range(n_col):
        ctx_out[b] = ctx[:, b * blk : (b + 1) * blk]
    ctx_copies = spread_out(4, lambda d: ctx_out.at[peer(d)], lambda d: ctx_in.at[d])
    total = ctx_out[c]
    for d, copy in enumerate(ctx_copies, 1):
        copy.wait_recv()
        total = total + ctx_in[d]
    gctx[c] = total * gate_b[c]
    gctx_copies = spread_out(5, lambda d: gctx.at[c], lambda d: gctx.at[c])
    for copy in gctx_copies:
        copy.wait_recv()
    out = None
    for b in range(n_col):
        piece = dot3(stacked(gctx[b]), *split(wout_ref[b * blk : (b + 1) * blk, :]), NN)
        out = piece if out is None else out + piece
    att_ref[...] = out

    for copy in tok_copies + back_copies + back_copies2 + stat_copies + ctx_copies + gctx_copies:
        copy.wait_send()
    for condition, copy in forwards:
        if condition is None:
            copy.wait_send()
        else:
            pl.when(condition)(copy.wait_send)


def pair_kernel(heads, pair_ref, ds_ref, pgain_ref, wbt_ref, grad_ref, weight_ref, wide_hi, wide_lo):
    channels = pair_ref.shape[2]
    keys = pair_ref.shape[1]

    @pl.when(pl.program_id(0) == 0)
    def _():
        hi, lo = split(wbt_ref[...] * pgain_ref[...])
        for ref, value in ((wide_hi, hi), (wide_lo, lo)):
            ref[...] = jnp.zeros_like(ref)
            for i in range(CHUNK):
                ref[heads * i : heads * (i + 1), channels * i : channels * (i + 1)] = value
        weight_ref[...] = jnp.zeros_like(weight_ref)

    x, scale = unit(pair_ref[...], channels)
    ds = ds_ref[...]
    across = jnp.concatenate([ds[i] for i in range(CHUNK)], axis=1)
    weight_ref[...] += dot3(stacked(across), *split(x.reshape(-1, channels)), NN)
    columns = ds.reshape(CHUNK * heads, keys).T
    d_unit = dot3(stacked(columns), wide_hi[...], wide_lo[...], NN)
    for i in range(CHUNK):
        d = d_unit[:, channels * i : channels * (i + 1)]
        centre = jnp.sum(d, axis=-1, keepdims=True) * (1.0 / channels)
        slope = jnp.sum(d * x[i], axis=-1, keepdims=True) * (1.0 / channels)
        grad_ref[i] = (d - centre - x[i] * slope) * scale[i]


def sum_kernel(n_row, n_col, part_ref, pgain_ref, out_ref, near, far, total, send_sem, recv_sem):
    r = lax.axis_index("row")
    c = lax.axis_index("col")
    greet(
        [{"row": (r + d) % n_row} for d in range(1, n_row)]
        + [{"col": (c + d) % n_col} for d in range(1, n_col)]
    )
    copies = []
    for d in range(1, n_row):
        copy = remote(
            part_ref, near.at[d], send_sem.at[d], recv_sem.at[d], row=(r + d) % n_row
        )
        copy.start()
        copies.append(copy)
    so_far = part_ref[...]
    for d, copy in enumerate(copies, 1):
        copy.wait_recv()
        so_far = so_far + near[d]
    total[...] = so_far
    later = []
    for d in range(1, n_col):
        k = n_row + d
        copy = remote(total, far.at[d], send_sem.at[k], recv_sem.at[k], col=(c + d) % n_col)
        copy.start()
        later.append(copy)
    for d, copy in enumerate(later, 1):
        copy.wait_recv()
        so_far = so_far + far[d]
    so_far = so_far * pgain_ref[...]
    heads, channels = so_far.shape
    square = jnp.concatenate([so_far, jnp.zeros((channels - heads, channels), F32)], axis=0)
    out_ref[...] = square.T[:, :heads]
    for copy in copies + later:
        copy.wait_send()


def local(
    n_row, n_col,
    single, pair, single_gain, pair_gain, w_query, w_key, w_value, w_gate, w_bias, w_out, cotangent
):
    tq, blk = single.shape
    width = single_gain.shape[0]
    channels, heads = w_bias.shape
    keys = pair.shape[1]
    n_chunk = tq // CHUNK
    vmem = pl.BlockSpec(memory_space=pltpu.VMEM)
    hbm = pl.BlockSpec(memory_space=pl.ANY)
    bits = (n_row // 2).bit_length() - 1
    w_bias_t = w_bias.T
    pair_gain = pair_gain.reshape(1, channels)
    single_gain = single_gain.reshape(1, width)
    blocks = pltpu.VMEM((n_col, tq, blk), F32)
    dma = pltpu.SemaphoreType.DMA
    attended, d_scores = pl.pallas_call(
        functools.partial(scores_kernel, n_row, n_col, heads),
        out_shape=(
            jax.ShapeDtypeStruct((tq, blk), F32),
            jax.ShapeDtypeStruct((tq, heads, keys), F32),
        ),
        in_specs=[vmem, hbm, vmem, vmem, hbm, hbm, hbm, hbm, vmem, vmem, vmem],
        out_specs=(vmem, vmem),
        scratch_shapes=[
            pltpu.VMEM(pair.shape, F32),
            *[pltpu.VMEM((width, width), F32)] * 4,
            blocks,
            pltpu.VMEM((2, n_col, tq, blk), F32),
            blocks, blocks, blocks,
            pltpu.VMEM((tq, heads, keys), F32),
            pltpu.VMEM((tq, heads, keys), F32),
            pltpu.VMEM((tq, width), F32),
            pltpu.VMEM((tq, width), F32),
            blocks,
            *[pltpu.VMEM((keys, width), BF16)] * 4,
            pltpu.VMEM((n_col, n_chunk, 8, CHUNK * heads), F32),
            pltpu.VMEM((tq, width), F32),
            blocks, blocks, blocks,
            dma((4,)), dma((n_chunk,)), dma((6, n_col)), dma((6, n_col)),
            dma((bits, n_col)), dma((n_col,)), dma((n_col,)), dma((n_col,)),
        ],
        compiler_params=pltpu.CompilerParams(
            collective_id=0, has_side_effects=True, vmem_limit_bytes=VMEM_LIMIT
        ),
        name="attend",
    )(
        single, pair, single_gain, pair_gain, w_query, w_key, w_value, w_gate, w_bias_t, w_out,
        cotangent,
    )
    whole = lambda shape: pl.BlockSpec(shape, lambda k: (0,) * len(shape))
    pair_grad, weight_part = pl.pallas_call(
        functools.partial(pair_kernel, heads),
        grid=(n_chunk,),
        out_shape=(
            jax.ShapeDtypeStruct(pair.shape, F32),
            jax.ShapeDtypeStruct((heads, channels), F32),
        ),
        in_specs=[
            pl.BlockSpec((CHUNK, keys, channels), lambda k: (k, 0, 0)),
            pl.BlockSpec((CHUNK, heads, keys), lambda k: (k, 0, 0)),
            whole((1, channels)),
            whole((heads, channels)),
        ],
        out_specs=(
            pl.BlockSpec((CHUNK, keys, channels), lambda k: (k, 0, 0)),
            whole((heads, channels)),
        ),
        scratch_shapes=[pltpu.VMEM((CHUNK * heads, CHUNK * channels), BF16)] * 2,
        compiler_params=pltpu.CompilerParams(vmem_limit_bytes=VMEM_LIMIT),
        name="pair_back",
    )(pair, d_scores, pair_gain, w_bias_t)
    bias_grad = pl.pallas_call(
        functools.partial(sum_kernel, n_row, n_col),
        out_shape=jax.ShapeDtypeStruct((channels, heads), F32),
        in_specs=[vmem, vmem],
        out_specs=vmem,
        scratch_shapes=[
            pltpu.VMEM((n_row, heads, channels), F32),
            pltpu.VMEM((n_col, heads, channels), F32),
            pltpu.VMEM((heads, channels), F32),
            dma((n_row + n_col,)), dma((n_row + n_col,)),
        ],
        compiler_params=pltpu.CompilerParams(collective_id=1, has_side_effects=True),
        name="sum_bias",
    )(weight_part, pair_gain)
    return (attended, pair_grad, bias_grad)


def solution(mesh):
    placed = (
        P("row", "col"),
        P("row", "col", None),
        P(),
        P(),
        P(),
        P(),
        P(),
        P(),
        P(),
        P(None, "col"),
        P("row", "col"),
    )
    return jax.shard_map(
        functools.partial(local, mesh.shape["row"], mesh.shape["col"]),
        mesh=mesh,
        in_specs=placed,
        out_specs=(P("row", "col"), P("row", "col", None), P()),
        check_vma=False,
    )
```

time: 233 us -> 86.8 us (0.37)
  blocking collectives: 116 us -> 0 us
  Pallas kernels: 0 us -> 80 us
  matrix products: 39.9 us -> 0 us
  other arithmetic: 27.5 us -> 0 us
  local copies, waits for them, and re-layouts: 23.7 us -> 5.62 us
  between operations: 15.7 us -> 0.66 us
  waiting for transfers between devices: 8.17 us -> 0 us
    pallas_call x0 -> x3, Pallas kernels: none -> 80 us  [the longest x1 58.2 us: local(): pl.pallas_call(functools.partial(scores_kernel, n_row, n_col, heads), out...]
    all_gather x4 -> x0, blocking collectives: 77.8 us -> none  [the longest x3 61.3 us: joined(): everything = jax.tree.map(lambda part: lax.all_gather(part, axis), array)]
    psum x1 -> x0, blocking collectives: 38.6 us -> none  [local(): bias_grad = lax.psum(weight_part, ('row', 'col'))]
    dot_general x11 -> x0, matrix products: 33.6 us -> none  [the longest x3 15.1 us: bias_of(): jnp.einsum('ijc,ch->ihj', layer_norm(pair_tile, pair_gain), weight, preci...]
    reduce_sum x7 -> x0, other arithmetic: 12.8 us -> none  [the longest x3 6.86 us: layer_norm(): spread = jnp.mean((values_in - centre) ** 2, axis=-1, keepdims=True)]
    unnamed x39 -> x5, local copies, waits for them, and re-layouts: 13 us -> 4.35 us
    add x6 -> x0, other arithmetic: 8.31 us -> none  [the longest x3 4.31 us: combine_parts(): acc_a * factor_a[:, :, None] + acc_b * factor_b[:, :, None]]
    all_gather x1 -> x0, waiting for transfers between devices: 8.12 us -> none  [local(): all_kv = lax.all_gather(kv_rows, 'row', axis=0, tiled=True)]
  transfers between devices with their start and end apart: 2 -> 0, of which waited for: 1 -> 0; matrix products, arithmetic and copies ran while one was open for 14% -> 0% of each run, Pallas kernels for 0% -> 0%
where the time goes in v1:
time: 86.8 us; the launch traced here: 86.3 us
  Pallas kernels  80 us (92%)
  local copies, waits for them, and re-layouts  5.62 us (6%)
    pallas_call x1, Pallas kernels, local(): pl.pallas_call(functools.partial(scores_kernel, n_row, n_col, heads), out...  58.2 us
    pallas_call x1, Pallas kernels, local(): pl.pallas_call(functools.partial(pair_kernel, heads), grid=(n_chunk,), ou...  11.2 us
    pallas_call x1, Pallas kernels, local(): pl.pallas_call(functools.partial(sum_kernel, n_row, n_col), out_shape=jax...  10.6 us
    unnamed x5, local copies, waits for them, and re-layouts  4.35 us

profile of v1, /device:TPU:0, one launch (start us, length us, event | category | flops | bytes accessed | tf_op | source)
XLA Modules:
  0.0 86.3 jit_solution(10215684977236396003)
XLA Ops:
  0.6 1.3 %reshape.12.gain_ref = f32[1,768]{1,0:T(1,128)} reshape(f32[768]{0:T(1024)} %param.13) | data formatting | bytes 6144 | tf_op jit(solution)/shard_map/reshape | solution.py:371
  1.9 2.2 %copy.14.wout_ref = f32[768,192]{1,0:T(8,128)} copy(f32[768,192]{0,1:T(8,128)} %param.20) | data formatting | bytes 1179648 | tf_op args[9]
  4.1 58.2 %attend.1 = (f32[64,192]{1,0:T(8,128)}, f32[64,16,128]{2,1,0:T(8,128)}) custom-call(f32[64,192]{1,0:T(8,128)} %single_ref.1, f32[64,128,128]{2,1,0:T(8,128)} %pair_ref.1, f32[1,768]{1,0:T(1,128)} %reshape.12.gain_ref, f32[1,128]{1,0:T(1,128)} %bitcast.4, f32[768,768]{1,0:T(8,128)} %wq_hbm.1, f32[768,768]{1,0:T(8,128)} %wk_hbm.1, f32[768,768]{1,0:T(8,128)} %wv_hbm.1, ...), custom_call_target="tpu_custom_call" | custom-call | tf_op jit(solution)/shard_map/attend/pallas_call | solution.py:374
  62.3 0.0 copy-start
  62.3 11.2 %pair_back.1 = (f32[64,128,128]{2,1,0:T(8,128)}, f32[16,128]{1,0:T(8,128)}) custom-call(f32[64,128,128]{2,1,0:T(8,128)} %pair_ref.1, f32[64,16,128]{2,1,0:T(8,128)} %get-tuple-element.8.ds_ref, f32[1,128]{1,0:T(1,128)} %bitcast.5, f32[16,128]{1,0:T(8,128)} %bitcast.3), custom_call_target="tpu_custom_call" | custom-call | tf_op jit(solution)/shard_map/pair_back/pallas_call | solution.py:409
  73.5 10.6 %sum_bias.1 = f32[128,16]{1,0:T(8,128)} custom-call(f32[16,128]{1,0:T(8,128)} %get-tuple-element.10.part_ref, f32[1,128]{1,0:T(1,128)} %bitcast.6), custom_call_target="tpu_custom_call" | custom-call | tf_op jit(solution)/shard_map/sum_bias/pallas_call | solution.py:430
  84.1 1.5 %copy.15 = f32[128,16]{0,1:T(8,128)} copy(f32[128,16]{1,0:T(8,128)} %sum_bias.1) | data formatting | bytes 16384
  85.6 0.0 copy-done
  85.6 0.6 copy.17
Async XLA Ops:
  62.3 23.3 %copy-start = (f32[64,192]{1,0:T(8,128)S(1)}, f32[64,192]{1,0:T(8,128)}, u32[]{:S(2)}) copy-start(f32[64,192]{1,0:T(8,128)} %get-tuple-element.17) | copy-start | bytes 147460

commit v2 on v1

v2 whole, which is shorter than its diff:
```python
import functools

import jax
import jax.numpy as jnp
from jax import lax
from jax.experimental import pallas as pl
from jax.experimental.pallas import tpu as pltpu
from jax.sharding import PartitionSpec as P

MESH = pl.DeviceIdType.MESH
VMEM_LIMIT = 56 * 1024 * 1024
CHUNK = 8
F32 = jnp.float32
BF16 = jnp.bfloat16
NN = (((1,), (0,)), ((), ()))
NT = (((1,), (1,)), ((), ()))


def split(x):
    hi = x.astype(BF16)
    return hi, (x - hi.astype(F32)).astype(BF16)


def stacked(x):
    return jnp.concatenate(split(x), axis=0)


def dot(a, b, dims):
    return lax.dot_general(a, b, dims, preferred_element_type=F32)


def dot3(both, b_hi, b_lo, dims):
    m = both.shape[0] // 2
    high = dot(both, b_hi, dims)
    return high[:m] + high[m:] + dot(both[:m], b_lo, dims)


def dot_rows(both, b_both):
    m, n = both.shape[0] // 2, b_both.shape[0] // 2
    out = dot(both, b_both, NT)
    return out[:m, :n] + (out[:m, n:] + out[m:, :n])


def dot_deep(x, b_both, b_hi):
    hi, lo = split(x)
    return dot(jnp.concatenate([hi, hi], axis=1), b_both, NN) + dot(lo, b_hi, NN)


def unit(x, width):
    centre = jnp.sum(x, axis=-1, keepdims=True) * (1.0 / width)
    x = x - centre
    spread = jnp.sum(x * x, axis=-1, keepdims=True) * (1.0 / width)
    scale = lax.rsqrt(spread + 1e-05)
    return x * scale, scale


def remote(src, dst, send_sem, recv_sem, **device):
    return pltpu.make_async_remote_copy(
        src_ref=src, dst_ref=dst, send_sem=send_sem, recv_sem=recv_sem,
        device_id=device, device_id_type=MESH,
    )


def greet(devices):
    barrier = pltpu.get_barrier_semaphore()
    for device in devices:
        pl.semaphore_signal(barrier, inc=1, device_id=device, device_id_type=MESH)
    pl.semaphore_wait(barrier, len(devices))


def layer_kernel(
    n_row, n_col, heads,
    single_ref, pair_hbm, gain_ref, pgain_ref, wq_hbm, wk_hbm, wv_hbm, wg_hbm, wbt_ref, wout_ref,
    cot_ref,
    att_ref, grad_hbm, bgrad_ref,
    pair_v, scale_v, wq_v, wk_v, wv_v, wg_v,
    tok, keyb, part_out, part_in, back, s_ref, dp_ref, q_ref, dc_ref, gate_b,
    kb, vb, stat, ctx_ref, ctx_out, ctx_in, gctx,
    w_hi, w_lo, wide_b, total_w, near, far,
    sum_send, sum_recv, o_sem, w_sem, p_sem, send_sem, recv_sem, tree_send, tree_recv, mate_send, mate_recv,
):
    r = lax.axis_index("row")
    c = lax.axis_index("col")
    tq, blk = single_ref.shape
    width = blk * n_col
    dim = width // heads
    n_chunk = tq // CHUNK
    n_chip = n_row // 2
    bits = n_chip.bit_length() - 1
    parity = r % 2
    chip = r // 2

    weights = [(wq_hbm, wq_v), (wg_hbm, wg_v), (wk_hbm, wk_v), (wv_hbm, wv_v)]
    pair_copies = [
        pltpu.make_async_copy(
            pair_hbm.at[pl.ds(CHUNK * k, CHUNK)], pair_v.at[pl.ds(CHUNK * k, CHUNK)], p_sem.at[k]
        )
        for k in range(n_chunk)
    ]
    weight_copies = [
        pltpu.make_async_copy(src, dst, w_sem.at[k]) for k, (src, dst) in enumerate(weights)
    ]
    for copy in pair_copies[:2] + weight_copies + pair_copies[2:]:
        copy.start()

    def peer(d):
        return (c + d) % n_col

    mate = r + 1 - 2 * parity
    chip_bits = [(chip // (1 << e)) % 2 for e in range(bits)]
    col_bits = [(c // (1 << e)) % 2 for e in range(bits)]
    away = [a + b - 2 * a * b for a, b in zip(chip_bits, col_bits)]
    beside = [r + (2 << e) * (1 - 2 * chip_bits[e]) for e in range(bits)]
    greet(
        [{"col": peer(d)} for d in range(1, n_col)]
        + [{"row": (r + d) % n_row} for d in range(1, n_row)]
    )

    def spread_out(stage, src_of, dst_of):
        copies = []
        for d in range(1, n_col):
            copy = remote(
                src_of(d), dst_of(d), send_sem.at[stage, d], recv_sem.at[stage, d], col=peer(d)
            )
            copy.start()
            copies.append(copy)
        return copies

    tok_copies = spread_out(0, lambda d: single_ref, lambda d: tok.at[c])
    tok[c] = single_ref[...]

    part = dot3(stacked(cot_ref[...]), *split(wout_ref[...]), NN)
    for b in range(n_col):
        part_out[b] = part[:, b * blk : (b + 1) * blk]
    back_copies = spread_out(1, lambda d: part_out.at[peer(d)], lambda d: part_in.at[d])
    gain = gain_ref[...].reshape(1, width)

    weight_t = wbt_ref[...] * pgain_ref[...]
    wb = stacked(weight_t)
    wb = jnp.concatenate([wb, jnp.concatenate([wb[:heads], jnp.zeros_like(wb[:heads])], 0)], 1)

    def pair_bias(k):
        pair_copies[k].wait()
        x = pair_v[pl.ds(CHUNK * k, CHUNK)]
        x, scale = unit(x, x.shape[-1])
        pair_v[pl.ds(CHUNK * k, CHUNK)] = x
        scale_v[pl.ds(CHUNK * k, CHUNK)] = jnp.broadcast_to(scale, x.shape)
        bias = dot(wb, jnp.concatenate(split(x.reshape(-1, x.shape[-1])), axis=1), NT)
        bias = bias[:heads] + bias[heads:]
        keys_here = s_ref.shape[2]
        for i in range(CHUNK):
            s_ref[CHUNK * k + i] = bias[:, i * keys_here : (i + 1) * keys_here]

    at_source = sum(away) == 0
    forwards = []
    for t in range(n_col):
        block = (c - t + n_col) % n_col
        if t:
            tok_copies[t - 1].wait_recv()

        @pl.when(at_source)
        def _():
            keyb[parity, block] = tok[block]

        @pl.when(jnp.logical_not(at_source))
        def _():
            remote(
                keyb.at[parity, block], keyb.at[parity, block], tree_send.at[0, t],
                tree_recv.at[t], row=mate,
            ).wait_recv()

        for e in reversed(range(bits)):
            copy = remote(
                keyb.at[parity, block], keyb.at[parity, block], tree_send.at[e, t],
                tree_recv.at[t], row=beside[e],
            )
            forwards.append((sum(away[: e + 1]) == 0, copy))
            pl.when(forwards[-1][0])(copy.start)
        copy = remote(
            keyb.at[parity, block], keyb.at[parity, block], mate_send.at[t], mate_recv.at[t],
            row=mate,
        )
        copy.start()
        forwards.append((None, copy))
        if t < n_col - 1:
            early = n_chunk - 3
            for k in range(t * early // (n_col - 1), (t + 1) * early // (n_col - 1)):
                pair_bias(k)

    for copy in back_copies:
        copy.wait_recv()
    total = part_out[c]
    for d in range(1, n_col):
        total = total + part_in[d]
    back[c] = total
    back_copies2 = spread_out(2, lambda d: back.at[c], lambda d: back.at[c])

    for k in range(n_chunk - 3, n_chunk):
        pair_bias(k)
    step = 256
    for k, (_, w_ref) in enumerate(weights):
        weight_copies[k].wait()
        for lo in range(0, width, step):
            w_hi[k, lo : lo + step], w_lo[k, lo : lo + step] = split(w_ref[lo : lo + step, :])
    wide_b[...] = jnp.zeros_like(wide_b)
    centred = weight_t - jnp.sum(weight_t, axis=1, keepdims=True) * (1.0 / weight_t.shape[1])
    channels = weight_t.shape[1]
    for half, value in enumerate(split(centred)):
        for i in range(CHUNK):
            row = half * CHUNK * heads + heads * i
            wide_b[row : row + heads, channels * i : channels * (i + 1)] = value

    def project(both, k):
        out = None
        for lo in range(0, width, step):
            piece = dot3(
                both[:, lo : lo + step], w_hi[k, lo : lo + step], w_lo[k, lo : lo + step], NN
            )
            out = piece if out is None else out + piece
        return out

    def joined(ref, *lead):
        return jnp.concatenate([ref[(*lead, b)] for b in range(n_col)], axis=1)

    rows = stacked(unit(joined(tok), width)[0] * gain)
    q_ref[...] = project(rows, 0) * dim ** (-0.5)
    gate = jax.nn.sigmoid(project(rows, 1))
    for b in range(n_col):
        gate_b[b] = gate[:, b * blk : (b + 1) * blk]

    for _, copy in forwards[bits :: bits + 1]:
        copy.wait_recv()
    tokens = jnp.concatenate([joined(keyb, 0), joined(keyb, 1)], axis=0)
    rows = stacked(unit(tokens, width)[0] * gain)
    kb[...] = stacked(project(rows, 2))
    vb[...] = stacked(project(rows, 3))

    for copy in back_copies2:
        copy.wait_recv()
    dc_ref[...] = joined(back) * gate

    head_of = lax.broadcasted_iota(jnp.int32, (heads, width), 0) * dim
    feature = lax.broadcasted_iota(jnp.int32, (heads, width), 1)
    mask = jnp.where((feature >= head_of) & (feature < head_of + dim), 1.0, 0.0)
    flat = CHUNK * heads

    def by_head(ref, k):
        x = ref[pl.ds(pl.multiple_of(CHUNK * k, CHUNK), CHUNK), :]
        return stacked((x[:, None, :] * mask[None]).reshape(flat, width))

    lane = lax.broadcasted_iota(jnp.int32, (flat, 128), 1)

    def forward(k, carry):
        here = pl.ds(CHUNK * k, CHUNK)
        s = s_ref[here].reshape(flat, -1)
        s = s + dot_rows(by_head(q_ref, k), kb[...])
        top = jnp.max(s, axis=-1, keepdims=True)
        expo = jnp.exp(s - top)
        dp = dot_rows(by_head(dc_ref, k), vb[...])
        sums = jnp.sum(expo, axis=-1, keepdims=True)
        delta = jnp.sum(expo * dp, axis=-1, keepdims=True)
        s_ref[here] = expo.reshape(CHUNK, heads, -1)
        dp_ref[here] = dp.reshape(CHUNK, heads, -1)
        packed = jnp.where(lane == 0, top, jnp.where(lane == 1, sums, delta))
        stat[c, k] = packed.T[:8]
        return carry

    lax.fori_loop(0, n_chunk, forward, 0)
    stat_copies = spread_out(3, lambda d: stat.at[c], lambda d: stat.at[c])
    for copy in stat_copies:
        copy.wait_recv()

    def backward(k, carry):
        here = pl.ds(CHUNK * k, CHUNK)
        every = [stat[b, k] for b in range(n_col)]
        top = functools.reduce(jnp.maximum, [x[0:1] for x in every])
        factors = [jnp.exp(x[0:1] - top) for x in every]
        sums = sum(f * x[1:2] for f, x in zip(factors, every))
        delta = sum(f * x[2:3] for f, x in zip(factors, every)) / sums
        mine = jnp.exp(stat[c, k][0:1] - top) / sums
        sub = lax.broadcasted_iota(jnp.int32, (128, flat), 0)
        columns = jnp.where(sub == 0, mine, delta).T
        probs = s_ref[here].reshape(flat, -1) * columns[:, 0:1]
        ds = probs * (dp_ref[here].reshape(flat, -1) - columns[:, 1:2])
        ds = ds.reshape(CHUNK, heads, -1)
        dp_ref[here] = ds
        across = jnp.concatenate([ds[i] for i in range(CHUNK)], axis=1)
        x_hi, x_lo = split(pair_v[here].reshape(-1, channels))
        both = dot(stacked(across), jnp.concatenate([x_hi, x_lo], axis=1), NN)
        carry = carry + (
            both[:heads, :channels] + (both[:heads, channels:] + both[heads:, :channels])
        )
        keys_here = vb.shape[0] // 2
        wide = dot_deep(probs, vb[...], vb[:keys_here]).reshape(CHUNK, heads, width)
        ctx_ref[pl.ds(pl.multiple_of(CHUNK * k, CHUNK), CHUNK), :] = jnp.sum(wide * mask[None], axis=1)
        return carry

    total_w[0] = lax.fori_loop(0, n_chunk, backward, jnp.zeros((heads, channels), F32))
    near_copies = []
    for d in range(1, n_row):
        copy = remote(
            total_w.at[0], near.at[d], sum_send.at[d], sum_recv.at[d], row=(r + d) % n_row
        )
        copy.start()
        near_copies.append(copy)
    ctx = ctx_ref[...]
    for b in range(n_col):
        ctx_out[b] = ctx[:, b * blk : (b + 1) * blk]
    ctx_copies = spread_out(4, lambda d: ctx_out.at[peer(d)], lambda d: ctx_in.at[d])

    def out_copy(k):
        here = pl.ds(CHUNK * k, CHUNK)
        return pltpu.make_async_copy(pair_v.at[here], grad_hbm.at[here], o_sem.at[k])

    def pair_back(k, carry):
        ds = dp_ref[pl.ds(CHUNK * k, CHUNK)]
        columns = ds.reshape(flat, -1).T
        d_unit = dot_deep(columns, wide_b[...], wide_b[:flat])
        for i in range(CHUNK):
            d = d_unit[:, channels * i : channels * (i + 1)]
            x = pair_v[CHUNK * k + i]
            slope = jnp.sum(d * x, axis=-1, keepdims=True) * (1.0 / channels)
            pair_v[CHUNK * k + i] = (d - x * slope) * scale_v[CHUNK * k + i]
        out_copy(k).start()
        return carry

    lax.fori_loop(0, n_chunk // 2, pair_back, 0)

    total = total_w[0]
    for d, copy in enumerate(near_copies, 1):
        copy.wait_recv()
        total = total + near[d]
    total_w[1] = total
    far_copies = []
    for d in range(1, n_col):
        k = n_row + d
        copy = remote(total_w.at[1], far.at[d], sum_send.at[k], sum_recv.at[k], col=peer(d))
        copy.start()
        far_copies.append(copy)
    total = ctx_out[c]
    for d, copy in enumerate(ctx_copies, 1):
        copy.wait_recv()
        total = total + ctx_in[d]
    gctx[c] = total * gate_b[c]
    gctx_copies = spread_out(5, lambda d: gctx.at[c], lambda d: gctx.at[c])

    lax.fori_loop(n_chunk // 2, n_chunk, pair_back, 0)

    total = total_w[1]
    for d, copy in enumerate(far_copies, 1):
        copy.wait_recv()
        total = total + far[d]
    bgrad_ref[...] = total * pgain_ref[...]
    for copy in gctx_copies:
        copy.wait_recv()
    att_ref[...] = dot3(stacked(joined(gctx)), *split(wout_ref[...]), NT)

    waits = tok_copies + back_copies + back_copies2 + stat_copies + ctx_copies + gctx_copies
    for copy in waits + near_copies + far_copies:
        copy.wait_send()
    for condition, copy in forwards:
        if condition is None:
            copy.wait_send()
        else:
            pl.when(condition)(copy.wait_send)
    for k in range(n_chunk):
        out_copy(k).wait()


def local(
    n_row, n_col,
    single, pair, single_gain, pair_gain, w_query, w_key, w_value, w_gate, w_bias, w_out, cotangent
):
    tq, blk = single.shape
    width = single_gain.shape[0]
    channels, heads = w_bias.shape
    keys = pair.shape[1]
    n_chunk = tq // CHUNK
    vmem = pl.BlockSpec(memory_space=pltpu.VMEM)
    hbm = pl.BlockSpec(memory_space=pl.ANY)
    bits = (n_row // 2).bit_length() - 1
    w_bias_t = w_bias.T
    pair_gain = pair_gain.reshape(1, channels)
    blocks = pltpu.VMEM((n_col, tq, blk), F32)
    dma = pltpu.SemaphoreType.DMA
    attended, pair_grad, bias_grad = pl.pallas_call(
        functools.partial(layer_kernel, n_row, n_col, heads),
        out_shape=(
            jax.ShapeDtypeStruct((tq, blk), F32),
            jax.ShapeDtypeStruct(pair.shape, F32),
            jax.ShapeDtypeStruct((heads, channels), F32),
        ),
        in_specs=[vmem, hbm, vmem, vmem, hbm, hbm, hbm, hbm, vmem, vmem, vmem],
        out_specs=(vmem, hbm, vmem),
        scratch_shapes=[
            pltpu.VMEM(pair.shape, F32),
            pltpu.VMEM(pair.shape, F32),
            *[pltpu.VMEM((width, width), F32)] * 4,
            blocks,
            pltpu.VMEM((2, n_col, tq, blk), F32),
            blocks, blocks, blocks,
            pltpu.VMEM((tq, heads, keys), F32),
            pltpu.VMEM((tq, heads, keys), F32),
            pltpu.VMEM((tq, width), F32),
            pltpu.VMEM((tq, width), F32),
            blocks,
            *[pltpu.VMEM((2 * keys, width), BF16)] * 2,
            pltpu.VMEM((n_col, n_chunk, 8, CHUNK * heads), F32),
            pltpu.VMEM((tq, width), F32),
            blocks, blocks, blocks,
            *[pltpu.VMEM((4, width, width), BF16)] * 2,
            pltpu.VMEM((2 * CHUNK * heads, CHUNK * channels), BF16),
            pltpu.VMEM((2, heads, channels), F32),
            pltpu.VMEM((n_row, heads, channels), F32),
            pltpu.VMEM((n_col, heads, channels), F32),
            dma((n_row + n_col,)), dma((n_row + n_col,)), dma((n_chunk,)),
            dma((4,)), dma((n_chunk,)), dma((6, n_col)), dma((6, n_col)),
            dma((bits, n_col)), dma((n_col,)), dma((n_col,)), dma((n_col,)),
        ],
        compiler_params=pltpu.CompilerParams(
            collective_id=0, has_side_effects=True, vmem_limit_bytes=VMEM_LIMIT
        ),
        name="layer",
    )(
        single, pair, single_gain, pair_gain, w_query, w_key, w_value, w_gate, w_bias_t, w_out.T,
        cotangent,
    )
    return (attended, pair_grad, bias_grad.T)


def solution(mesh):
    placed = (
        P("row", "col"),
        P("row", "col", None),
        P(),
        P(),
        P(),
        P(),
        P(),
        P(),
        P(),
        P(None, "col"),
        P("row", "col"),
    )
    return jax.shard_map(
        functools.partial(local, mesh.shape["row"], mesh.shape["col"]),
        mesh=mesh,
        in_specs=placed,
        out_specs=(P("row", "col"), P("row", "col", None), P()),
        check_vma=False,
    )
```

time: 86.8 us -> 67.2 us (0.77)
  Pallas kernels: 80 us -> 59.5 us
  local copies, waits for them, and re-layouts: 5.62 us -> 6.79 us
    pallas_call x3 -> x1, Pallas kernels: 80 us -> 59.5 us  [local(): pl.pallas_call(functools.partial(layer_kernel, n_row, n_col, heads), out_...]
    unnamed x5, local copies, waits for them, and re-layouts: 4.35 us -> 6.79 us
    reshape x1 -> x0, local copies, waits for them, and re-layouts: 1.27 us -> none  [local(): single_gain = single_gain.reshape(1, width)]
where the time goes in v2:
time: 67.2 us; the launch traced here: 67 us
  Pallas kernels  59.5 us (89%)
  local copies, waits for them, and re-layouts  6.79 us (10%)
    pallas_call x1, Pallas kernels, local(): pl.pallas_call(functools.partial(layer_kernel, n_row, n_col, heads), out_...  59.5 us
    unnamed x5, local copies, waits for them, and re-layouts  6.79 us

profile of v2, /device:TPU:0, one launch (start us, length us, event | category | flops | bytes accessed | tf_op | source)
XLA Modules:
  0.0 67.0 jit_solution(1136642694858785056)
XLA Ops:
  0.6 59.5 %layer.1 = (f32[64,192]{1,0:T(8,128)}, f32[64,128,128]{2,1,0:T(8,128)}, f32[16,128]{1,0:T(8,128)}) custom-call(f32[64,192]{1,0:T(8,128)} %single_ref.1, f32[64,128,128]{2,1,0:T(8,128)} %pair_hbm.1, f32[768]{0:T(1024)} %gain_ref.1, f32[1,128]{1,0:T(1,128)} %bitcast.7, f32[768,768]{1,0:T(8,128)} %wq_hbm.1, f32[768,768]{1,0:T(8,128)} %wk_hbm.1, ...), custom_call_target="tpu_custom_call" | custom-call | tf_op jit(solution)/shard_map/layer/pallas_call | solution.py:386
  60.2 1.5 %copy.17 = f32[64,192]{1,0:T(8,128)} copy(f32[64,192]{1,0:T(8,128)} %get-tuple-element.12) | data formatting | bytes 98304
  61.6 0.0 copy-start
  61.6 4.7 %copy.18 = f32[64,128,128]{2,1,0:T(8,128)} copy(f32[64,128,128]{2,1,0:T(8,128)} %get-tuple-element.13) | data formatting | bytes 8388608
  66.4 0.0 copy-done
  66.4 0.6 copy.19
Async XLA Ops:
  61.6 4.7 %copy-start = (f32[16,128]{1,0:T(8,128)S(1)}, f32[16,128]{1,0:T(8,128)}, u32[]{:S(2)}) copy-start(f32[16,128]{1,0:T(8,128)} %get-tuple-element.8) | copy-start | bytes 24580

commit v3 on v2

--- a/solution.py
+++ b/solution.py
@@ -8,7 +8,7 @@
 from jax.sharding import PartitionSpec as P
 
 MESH = pl.DeviceIdType.MESH
-VMEM_LIMIT = 56 * 1024 * 1024
+VMEM_LIMIT = 48 * 1024 * 1024
 CHUNK = 8
 F32 = jnp.float32
 BF16 = jnp.bfloat16
@@ -72,12 +72,12 @@
     n_row, n_col, heads,
     single_ref, pair_hbm, gain_ref, pgain_ref, wq_hbm, wk_hbm, wv_hbm, wg_hbm, wbt_ref, wout_ref,
     cot_ref,
-    att_ref, grad_hbm, bgrad_ref,
+    att_ref, grad_ref, bgrad_ref,
     pair_v, scale_v, wq_v, wk_v, wv_v, wg_v,
     tok, keyb, part_out, part_in, back, s_ref, dp_ref, q_ref, dc_ref, gate_b,
     kb, vb, stat, ctx_ref, ctx_out, ctx_in, gctx,
-    w_hi, w_lo, wide_b, total_w, near, far,
-    sum_send, sum_recv, o_sem, w_sem, p_sem, send_sem, recv_sem, tree_send, tree_recv, mate_send, mate_recv,
+    w_hi, w_lo, wide_b, total_w, near, far, factor,
+    sum_send, sum_recv, w_sem, p_sem, send_sem, recv_sem, tree_send, tree_recv, mate_send, mate_recv,
 ):
     r = lax.axis_index("row")
     c = lax.axis_index("col")
@@ -132,7 +132,6 @@
     part = dot3(stacked(cot_ref[...]), *split(wout_ref[...]), NN)
     for b in range(n_col):
         part_out[b] = part[:, b * blk : (b + 1) * blk]
-    back_copies = spread_out(1, lambda d: part_out.at[peer(d)], lambda d: part_in.at[d])
     gain = gain_ref[...].reshape(1, width)
 
     weight_t = wbt_ref[...] * pgain_ref[...]
@@ -182,6 +181,8 @@
         )
         copy.start()
         forwards.append((None, copy))
+        if t == n_col - 2:
+            back_copies = spread_out(1, lambda d: part_out.at[peer(d)], lambda d: part_in.at[d])
         if t < n_col - 1:
             early = n_chunk - 3
             for k in range(t * early // (n_col - 1), (t + 1) * early // (n_col - 1)):
@@ -267,6 +268,22 @@
 
     lax.fori_loop(0, n_chunk, forward, 0)
     stat_copies = spread_out(3, lambda d: stat.at[c], lambda d: stat.at[c])
+    keys_here = vb.shape[0] // 2
+
+    def weigh(k, carry):
+        expo = s_ref[pl.ds(CHUNK * k, CHUNK)].reshape(flat, -1)
+        wide = dot_deep(expo, vb[...], vb[:keys_here]).reshape(CHUNK, heads, width)
+        ctx_ref[pl.ds(pl.multiple_of(CHUNK * k, CHUNK), CHUNK), :] = jnp.sum(wide * mask[None], axis=1)
+        return carry
+
+    lax.fori_loop(0, n_chunk, weigh, 0)
+    ctx = ctx_ref[...]
+    for b in range(n_col):
+        ctx_out[b] = ctx[:, b * blk : (b + 1) * blk]
+    ctx_copies = spread_out(4, lambda d: ctx_out.at[peer(d)], lambda d: ctx_in.at[d])
+    own_head = lax.broadcasted_iota(jnp.int32, (heads, blk), 0) * dim
+    own_feature = lax.broadcasted_iota(jnp.int32, (heads, blk), 1) + c * blk
+    own_mask = jnp.where((own_feature >= own_head) & (own_feature < own_head + dim), 1.0, 0.0)
     for copy in stat_copies:
         copy.wait_recv()
 
@@ -279,7 +296,15 @@
         delta = sum(f * x[2:3] for f, x in zip(factors, every)) / sums
         mine = jnp.exp(stat[c, k][0:1] - top) / sums
         sub = lax.broadcasted_iota(jnp.int32, (128, flat), 0)
-        columns = jnp.where(sub == 0, mine, delta).T
+        columns = jnp.where(sub == 0, mine, delta)
+        sources = [stat[peer(n_col - d), k][0:1] for d in range(n_col)]
+        for d, x in enumerate(sources):
+            columns = jnp.where(sub == 2 + d, jnp.exp(x - top) / sums, columns)
+        columns = columns.T
+        for d in range(n_col):
+            weight = columns[:, 2 + d : 3 + d].reshape(CHUNK, heads, 1) * own_mask[None]
+            rows_here = pl.ds(pl.multiple_of(CHUNK * k, CHUNK), CHUNK)
+            factor[d, rows_here, :] = jnp.sum(weight, axis=1)
         probs = s_ref[here].reshape(flat, -1) * columns[:, 0:1]
         ds = probs * (dp_ref[here].reshape(flat, -1) - columns[:, 1:2])
         ds = ds.reshape(CHUNK, heads, -1)
@@ -290,9 +315,6 @@
         carry = carry + (
             both[:heads, :channels] + (both[:heads, channels:] + both[heads:, :channels])
         )
-        keys_here = vb.shape[0] // 2
-        wide = dot_deep(probs, vb[...], vb[:keys_here]).reshape(CHUNK, heads, width)
-        ctx_ref[pl.ds(pl.multiple_of(CHUNK * k, CHUNK), CHUNK), :] = jnp.sum(wide * mask[None], axis=1)
         return carry
 
     total_w[0] = lax.fori_loop(0, n_chunk, backward, jnp.zeros((heads, channels), F32))
@@ -303,14 +325,12 @@
         )
         copy.start()
         near_copies.append(copy)
-    ctx = ctx_ref[...]
-    for b in range(n_col):
-        ctx_out[b] = ctx[:, b * blk : (b + 1) * blk]
-    ctx_copies = spread_out(4, lambda d: ctx_out.at[peer(d)], lambda d: ctx_in.at[d])
-
-    def out_copy(k):
-        here = pl.ds(CHUNK * k, CHUNK)
-        return pltpu.make_async_copy(pair_v.at[here], grad_hbm.at[here], o_sem.at[k])
+    total = ctx_out[c] * factor[0]
+    for d, copy in enumerate(ctx_copies, 1):
+        copy.wait_recv()
+        total = total + ctx_in[d] * factor[d]
+    gctx[c] = total * gate_b[c]
+    gctx_copies = spread_out(5, lambda d: gctx.at[c], lambda d: gctx.at[c])
 
     def pair_back(k, carry):
         ds = dp_ref[pl.ds(CHUNK * k, CHUNK)]
@@ -320,8 +340,7 @@
             d = d_unit[:, channels * i : channels * (i + 1)]
             x = pair_v[CHUNK * k + i]
             slope = jnp.sum(d * x, axis=-1, keepdims=True) * (1.0 / channels)
-            pair_v[CHUNK * k + i] = (d - x * slope) * scale_v[CHUNK * k + i]
-        out_copy(k).start()
+            grad_ref[CHUNK * k + i] = (d - x * slope) * scale_v[CHUNK * k + i]
         return carry
 
     lax.fori_loop(0, n_chunk // 2, pair_back, 0)
@@ -337,13 +356,6 @@
         copy = remote(total_w.at[1], far.at[d], sum_send.at[k], sum_recv.at[k], col=peer(d))
         copy.start()
         far_copies.append(copy)
-    total = ctx_out[c]
-    for d, copy in enumerate(ctx_copies, 1):
-        copy.wait_recv()
-        total = total + ctx_in[d]
-    gctx[c] = total * gate_b[c]
-    gctx_copies = spread_out(5, lambda d: gctx.at[c], lambda d: gctx.at[c])
-
     lax.fori_loop(n_chunk // 2, n_chunk, pair_back, 0)
 
     total = total_w[1]
@@ -363,8 +375,18 @@
             copy.wait_send()
         else:
             pl.when(condition)(copy.wait_send)
-    for k in range(n_chunk):
-        out_copy(k).wait()
+
+
+def write_kernel(*refs):
+    count = len(refs) // 2
+    copies = [
+        pltpu.make_async_copy(src, dst, refs[-1].at[k])
+        for k, (src, dst) in enumerate(zip(refs[:count], refs[count:-1]))
+    ]
+    for copy in copies:
+        copy.start()
+    for copy in copies:
+        copy.wait()
 
 
 def local(
@@ -386,12 +408,12 @@
     attended, pair_grad, bias_grad = pl.pallas_call(
         functools.partial(layer_kernel, n_row, n_col, heads),
         out_shape=(
-            jax.ShapeDtypeStruct((tq, blk), F32),
-            jax.ShapeDtypeStruct(pair.shape, F32),
-            jax.ShapeDtypeStruct((heads, channels), F32),
+            pltpu.VMEM((tq, blk), F32),
+            pltpu.VMEM(pair.shape, F32),
+            pltpu.VMEM((heads, channels), F32),
         ),
         in_specs=[vmem, hbm, vmem, vmem, hbm, hbm, hbm, hbm, vmem, vmem, vmem],
-        out_specs=(vmem, hbm, vmem),
+        out_specs=(vmem,) * 3,
         scratch_shapes=[
             pltpu.VMEM(pair.shape, F32),
             pltpu.VMEM(pair.shape, F32),
@@ -413,7 +435,8 @@
             pltpu.VMEM((2, heads, channels), F32),
             pltpu.VMEM((n_row, heads, channels), F32),
             pltpu.VMEM((n_col, heads, channels), F32),
-            dma((n_row + n_col,)), dma((n_row + n_col,)), dma((n_chunk,)),
+            blocks,
+            dma((n_row + n_col,)), dma((n_row + n_col,)),
             dma((4,)), dma((n_chunk,)), dma((6, n_col)), dma((6, n_col)),
             dma((bits, n_col)), dma((n_col,)), dma((n_col,)), dma((n_col,)),
         ],
@@ -425,6 +448,16 @@
         single, pair, single_gain, pair_gain, w_query, w_key, w_value, w_gate, w_bias_t, w_out.T,
         cotangent,
     )
+    results = (attended, pair_grad, bias_grad)
+    attended, pair_grad, bias_grad = pl.pallas_call(
+        write_kernel,
+        out_shape=tuple(jax.ShapeDtypeStruct(x.shape, F32) for x in results),
+        in_specs=[vmem] * 3,
+        out_specs=(hbm,) * 3,
+        scratch_shapes=[dma((3,))],
+        compiler_params=pltpu.CompilerParams(vmem_limit_bytes=1024 * 1024),
+        name="write_out",
+    )(*[pltpu.with_memory_space_constraint(x, pltpu.VMEM) for x in results])
     return (attended, pair_grad, bias_grad.T)
 
 

time: 67.2 us -> 60 us (0.89)
  Pallas kernels: 59.5 us -> 54.2 us
  local copies, waits for them, and re-layouts: 6.79 us -> 4.77 us
    pallas_call x1, Pallas kernels: 59.5 us -> 52.1 us  [local(): pl.pallas_call(functools.partial(layer_kernel, n_row, n_col, heads), out_...]
    pallas_call x0 -> x1, Pallas kernels: none -> 2.07 us  [local(): pl.pallas_call(write_kernel, out_shape=tuple((jax.ShapeDtypeStruct(x.shap...]
    unnamed x5 -> x12, local copies, waits for them, and re-layouts: 6.79 us -> 4.77 us
where the time goes in v3:
time: 60 us; the launch traced here: 59.6 us
  Pallas kernels  54.2 us (90%)
  local copies, waits for them, and re-layouts  4.77 us (8%)
  between operations  0.66 us (1%)
    pallas_call x1, Pallas kernels, local(): pl.pallas_call(functools.partial(layer_kernel, n_row, n_col, heads), out_...  52.1 us
    unnamed x12, local copies, waits for them, and re-layouts  4.77 us
    pallas_call x1, Pallas kernels, local(): pl.pallas_call(write_kernel, out_shape=tuple((jax.ShapeDtypeStruct(x.shap...  2.07 us

profile of v3, /device:TPU:0, one launch (start us, length us, event | category | flops | bytes accessed | tf_op | source)
XLA Modules:
  0.0 59.6 jit_solution(9290952283707150524)
XLA Ops:
  0.6 0.0 copy-start
  0.6 1.1 %copy-done = f32[768,192]{0,1:T(8,128)S(1)} copy-done((f32[768,192]{0,1:T(8,128)S(1)}, f32[768,192]{0,1:T(8,128)}, u32[]{:S(2)}) %copy-start) | copy-done | bytes 589848
  1.7 0.0 copy-start.1
  1.7 0.8 %copy-done.1 = f32[64,192]{1,0:T(8,128)S(1)} copy-done((f32[64,192]{1,0:T(8,128)S(1)}, f32[64,192]{1,0:T(8,128)}, u32[]{:S(2)}) %copy-start.1) | copy-done | bytes 49176
  2.5 0.0 copy-start.2
  2.5 0.8 %copy-done.2 = f32[64,192]{1,0:T(8,128)S(1)} copy-done((f32[64,192]{1,0:T(8,128)S(1)}, f32[64,192]{1,0:T(8,128)}, u32[]{:S(2)}) %copy-start.2) | copy-done | bytes 49176
  3.4 0.0 copy-start.3
  3.4 0.7 %copy-done.3 = f32[128,16]{0,1:T(8,128)S(1)} copy-done((f32[128,16]{0,1:T(8,128)S(1)}, f32[128,16]{0,1:T(8,128)}, u32[]{:S(2)}) %copy-start.3) | copy-done | bytes 8216
  4.1 0.0 copy-start.4
  4.1 0.7 %copy-done.4 = f32[768]{0:T(1024)S(1)} copy-done((f32[768]{0:T(1024)S(1)}, f32[768]{0:T(1024)}, u32[]{:S(2)}) %copy-start.4) | copy-done | bytes 3096
  4.8 0.0 copy-start.5
  4.8 0.7 %copy-done.5 = f32[128]{0:T(128)S(1)} copy-done((f32[128]{0:T(128)S(1)}, f32[128]{0:T(128)}, u32[]{:S(2)}) %copy-start.5) | copy-done | bytes 536
  5.4 52.1 %layer.1 = (f32[64,192]{1,0:T(8,128)S(1)}, f32[64,128,128]{2,1,0:T(8,128)S(1)}, f32[16,128]{1,0:T(8,128)S(1)}) custom-call(f32[64,192]{1,0:T(8,128)S(1)} %copy-done.1, f32[64,128,128]{2,1,0:T(8,128)} %pair_hbm.1, f32[768]{0:T(1024)S(1)} %copy-done.4, f32[1,128]{1,0:T(1,128)S(1)} %bitcast.6, f32[768,768]{1,0:T(8,128)} %wq_hbm.1, f32[768,768]{1,0:T(8,128)} %wk_hbm.1, ...), custom_call_target="tpu_custom_call" | custom-call | tf_op jit(solution)/shard_map/layer/pallas_call | solution.py:408
  57.6 2.1 %write_out.1 = (f32[64,192]{1,0:T(8,128)}, f32[64,128,128]{2,1,0:T(8,128)}, f32[16,128]{1,0:T(8,128)}) custom-call(f32[64,192]{1,0:T(8,128)S(1)} %get-tuple-element.9.refs_0_, f32[64,128,128]{2,1,0:T(8,128)S(1)} %get-tuple-element.10.refs_1_, f32[16,128]{1,0:T(8,128)S(1)} %get-tuple-element.11.refs_2_), custom_call_target="tpu_custom_call" | custom-call | tf_op jit(solution)/shard_map/write_out/pallas_call | solution.py:452
Async XLA Ops:
  0.6 1.1 %copy-start = (f32[768,192]{0,1:T(8,128)S(1)}, f32[768,192]{0,1:T(8,128)}, u32[]{:S(2)}) copy-start(f32[768,192]{0,1:T(8,128)} %param.20) | copy-start | bytes 1769476
  1.7 0.8 %copy-start.1 = (f32[64,192]{1,0:T(8,128)S(1)}, f32[64,192]{1,0:T(8,128)}, u32[]{:S(2)}) copy-start(f32[64,192]{1,0:T(8,128)} %single_ref.1) | copy-start | bytes 147460
  2.5 0.8 %copy-start.2 = (f32[64,192]{1,0:T(8,128)S(1)}, f32[64,192]{1,0:T(8,128)}, u32[]{:S(2)}) copy-start(f32[64,192]{1,0:T(8,128)} %cot_ref.1) | copy-start | bytes 147460
  3.4 0.7 %copy-start.3 = (f32[128,16]{0,1:T(8,128)S(1)}, f32[128,16]{0,1:T(8,128)}, u32[]{:S(2)}) copy-start(f32[128,16]{0,1:T(8,128)} %param.19) | copy-start | bytes 24580
  4.1 0.7 %copy-start.4 = (f32[768]{0:T(1024)S(1)}, f32[768]{0:T(1024)}, u32[]{:S(2)}) copy-start(f32[768]{0:T(1024)} %gain_ref.1) | copy-start | bytes 9220
  4.8 0.7 %copy-start.5 = (f32[128]{0:T(128)S(1)}, f32[128]{0:T(128)}, u32[]{:S(2)}) copy-start(f32[128]{0:T(128)} %param.14) | copy-start | bytes 1540

commit v4 on v3

--- a/solution.py
+++ b/solution.py
@@ -68,20 +68,30 @@
     pl.semaphore_wait(barrier, len(devices))
 
 
+def in_pairs(start, stop, body, carry):
+    def two(k, carry):
+        for u in range(2):
+            carry = body(2 * k + u, carry)
+        return carry
+
+    return lax.fori_loop(start // 2, stop // 2, two, carry)
+
+
 def layer_kernel(
     n_row, n_col, heads,
-    single_ref, pair_hbm, gain_ref, pgain_ref, wq_hbm, wk_hbm, wv_hbm, wg_hbm, wbt_ref, wout_ref,
-    cot_ref,
+    single_hbm, pair_hbm, gain_hbm, pgain_hbm, wq_hbm, wk_hbm, wv_hbm, wg_hbm, wbt_hbm, wout_hbm,
+    cot_hbm,
     att_ref, grad_ref, bgrad_ref,
     pair_v, scale_v, wq_v, wk_v, wv_v, wg_v,
     tok, keyb, part_out, part_in, back, s_ref, dp_ref, q_ref, dc_ref, gate_b,
     kb, vb, stat, ctx_ref, ctx_out, ctx_in, gctx,
     w_hi, w_lo, wide_b, total_w, near, far, factor,
-    sum_send, sum_recv, w_sem, p_sem, send_sem, recv_sem, tree_send, tree_recv, mate_send, mate_recv,
+    cot_ref, wout_ref, wbt_ref, pgain_ref, gain_ref,
+    i_sem, sum_send, sum_recv, w_sem, p_sem, send_sem, recv_sem, tree_send, tree_recv, mate_send, mate_recv,
 ):
     r = lax.axis_index("row")
     c = lax.axis_index("col")
-    tq, blk = single_ref.shape
+    tq, blk = single_hbm.shape
     width = blk * n_col
     dim = width // heads
     n_chunk = tq // CHUNK
@@ -100,7 +110,14 @@
     weight_copies = [
         pltpu.make_async_copy(src, dst, w_sem.at[k]) for k, (src, dst) in enumerate(weights)
     ]
-    for copy in pair_copies[:2] + weight_copies + pair_copies[2:]:
+    small = [
+        (single_hbm, tok.at[c]), (cot_hbm, cot_ref), (wout_hbm, wout_ref),
+        (wbt_hbm, wbt_ref), (pgain_hbm, pgain_ref), (gain_hbm, gain_ref),
+    ]
+    small_copies = [
+        pltpu.make_async_copy(src, dst, i_sem.at[k]) for k, (src, dst) in enumerate(small)
+    ]
+    for copy in small_copies + pair_copies[:2] + weight_copies + pair_copies[2:]:
         copy.start()
 
     def peer(d):
@@ -126,8 +143,10 @@
             copies.append(copy)
         return copies
 
-    tok_copies = spread_out(0, lambda d: single_ref, lambda d: tok.at[c])
-    tok[c] = single_ref[...]
+    small_copies[0].wait()
+    tok_copies = spread_out(0, lambda d: tok.at[c], lambda d: tok.at[c])
+    for copy in small_copies[1:]:
+        copy.wait()
 
     part = dot3(stacked(cot_ref[...]), *split(wout_ref[...]), NN)
     for b in range(n_col):
@@ -266,7 +285,7 @@
         stat[c, k] = packed.T[:8]
         return carry
 
-    lax.fori_loop(0, n_chunk, forward, 0)
+    in_pairs(0, n_chunk, forward, 0)
     stat_copies = spread_out(3, lambda d: stat.at[c], lambda d: stat.at[c])
     keys_here = vb.shape[0] // 2
 
@@ -276,7 +295,7 @@
         ctx_ref[pl.ds(pl.multiple_of(CHUNK * k, CHUNK), CHUNK), :] = jnp.sum(wide * mask[None], axis=1)
         return carry
 
-    lax.fori_loop(0, n_chunk, weigh, 0)
+    in_pairs(0, n_chunk, weigh, 0)
     ctx = ctx_ref[...]
     for b in range(n_col):
         ctx_out[b] = ctx[:, b * blk : (b + 1) * blk]
@@ -317,7 +336,7 @@
         )
         return carry
 
-    total_w[0] = lax.fori_loop(0, n_chunk, backward, jnp.zeros((heads, channels), F32))
+    total_w[0] = in_pairs(0, n_chunk, backward, jnp.zeros((heads, channels), F32))
     near_copies = []
     for d in range(1, n_row):
         copy = remote(
@@ -343,7 +362,7 @@
             grad_ref[CHUNK * k + i] = (d - x * slope) * scale_v[CHUNK * k + i]
         return carry
 
-    lax.fori_loop(0, n_chunk // 2, pair_back, 0)
+    in_pairs(0, n_chunk // 2, pair_back, 0)
 
     total = total_w[0]
     for d, copy in enumerate(near_copies, 1):
@@ -356,7 +375,7 @@
         copy = remote(total_w.at[1], far.at[d], sum_send.at[k], sum_recv.at[k], col=peer(d))
         copy.start()
         far_copies.append(copy)
-    lax.fori_loop(n_chunk // 2, n_chunk, pair_back, 0)
+    in_pairs(n_chunk // 2, n_chunk, pair_back, 0)
 
     total = total_w[1]
     for d, copy in enumerate(far_copies, 1):
@@ -399,7 +418,7 @@
     keys = pair.shape[1]
     n_chunk = tq // CHUNK
     vmem = pl.BlockSpec(memory_space=pltpu.VMEM)
-    hbm = pl.BlockSpec(memory_space=pl.ANY)
+    hbm = pl.BlockSpec(memory_space=pltpu.HBM)
     bits = (n_row // 2).bit_length() - 1
     w_bias_t = w_bias.T
     pair_gain = pair_gain.reshape(1, channels)
@@ -412,7 +431,7 @@
             pltpu.VMEM(pair.shape, F32),
             pltpu.VMEM((heads, channels), F32),
         ),
-        in_specs=[vmem, hbm, vmem, vmem, hbm, hbm, hbm, hbm, vmem, vmem, vmem],
+        in_specs=[hbm] * 11,
         out_specs=(vmem,) * 3,
         scratch_shapes=[
             pltpu.VMEM(pair.shape, F32),
@@ -436,6 +455,12 @@
             pltpu.VMEM((n_row, heads, channels), F32),
             pltpu.VMEM((n_col, heads, channels), F32),
             blocks,
+            pltpu.VMEM((tq, blk), F32),
+            pltpu.VMEM((blk, width), F32),
+            pltpu.VMEM((heads, channels), F32),
+            pltpu.VMEM((1, channels), F32),
+            pltpu.VMEM((width,), F32),
+            dma((6,)),
             dma((n_row + n_col,)), dma((n_row + n_col,)),
             dma((4,)), dma((n_chunk,)), dma((6, n_col)), dma((6, n_col)),
             dma((bits, n_col)), dma((n_col,)), dma((n_col,)), dma((n_col,)),
@@ -445,8 +470,13 @@
         ),
         name="layer",
     )(
-        single, pair, single_gain, pair_gain, w_query, w_key, w_value, w_gate, w_bias_t, w_out.T,
-        cotangent,
+        *[
+            pltpu.with_memory_space_constraint(x, pltpu.HBM)
+            for x in (
+                single, pair, single_gain, pair_gain, w_query, w_key, w_value, w_gate, w_bias_t,
+                w_out.T, cotangent,
+            )
+        ]
     )
     results = (attended, pair_grad, bias_grad)
     attended, pair_grad, bias_grad = pl.pallas_call(

time: 60 us -> 54.4 us (0.907)
  local copies, waits for them, and re-layouts: 4.77 us -> 0 us
  Pallas kernels: 54.2 us -> 53.6 us
    unnamed x12 -> x0, local copies, waits for them, and re-layouts: 4.77 us -> none
where the time goes in v4:
time: 54.4 us; the launch traced here: 54.2 us
  Pallas kernels  53.6 us (99%)
  between operations  0.64 us (1%)
    pallas_call x1, Pallas kernels, local(): pl.pallas_call(functools.partial(layer_kernel, n_row, n_col, heads), out_...  51.5 us
    pallas_call x1, Pallas kernels, local(): pl.pallas_call(write_kernel, out_shape=tuple((jax.ShapeDtypeStruct(x.shap...  2.07 us

profile of v4, /device:TPU:0, one launch (start us, length us, event | category | flops | bytes accessed | tf_op | source)
XLA Modules:
  0.0 54.2 jit_solution(17654251829378387474)
XLA Ops:
  0.6 51.5 %layer.1 = (f32[64,192]{1,0:T(8,128)S(1)}, f32[64,128,128]{2,1,0:T(8,128)S(1)}, f32[16,128]{1,0:T(8,128)S(1)}) custom-call(f32[64,192]{1,0:T(8,128)} %single_hbm.1, f32[64,128,128]{2,1,0:T(8,128)} %pair_hbm.1, f32[768]{0:T(1024)} %gain_hbm.1, f32[1,128]{1,0:T(1,128)} %bitcast.6, f32[768,768]{1,0:T(8,128)} %wq_hbm.1, f32[768,768]{1,0:T(8,128)} %wk_hbm.1, ...), custom_call_target="tpu_custom_call" | custom-call | tf_op jit(solution)/shard_map/layer/pallas_call | solution.py:427
  52.2 2.1 %write_out.1 = (f32[64,192]{1,0:T(8,128)}, f32[64,128,128]{2,1,0:T(8,128)}, f32[16,128]{1,0:T(8,128)}) custom-call(f32[64,192]{1,0:T(8,128)S(1)} %get-tuple-element.9.refs_0_, f32[64,128,128]{2,1,0:T(8,128)S(1)} %get-tuple-element.10.refs_1_, f32[16,128]{1,0:T(8,128)S(1)} %get-tuple-element.11.refs_2_), custom_call_target="tpu_custom_call" | custom-call | tf_op jit(solution)/shard_map/write_out/pallas_call | solution.py:482

commit v5 on v4

--- a/solution.py
+++ b/solution.py
@@ -170,6 +170,7 @@
             s_ref[CHUNK * k + i] = bias[:, i * keys_here : (i + 1) * keys_here]
 
     at_source = sum(away) == 0
+    early = min(n_col - 1, n_chunk)
     forwards = []
     for t in range(n_col):
         block = (c - t + n_col) % n_col
@@ -203,7 +204,6 @@
         if t == n_col - 2:
             back_copies = spread_out(1, lambda d: part_out.at[peer(d)], lambda d: part_in.at[d])
         if t < n_col - 1:
-            early = n_chunk - 3
             for k in range(t * early // (n_col - 1), (t + 1) * early // (n_col - 1)):
                 pair_bias(k)
 
@@ -215,7 +215,7 @@
     back[c] = total
     back_copies2 = spread_out(2, lambda d: back.at[c], lambda d: back.at[c])
 
-    for k in range(n_chunk - 3, n_chunk):
+    for k in range(early, n_chunk):
         pair_bias(k)
     step = 256
     for k, (_, w_ref) in enumerate(weights):

time: 54.4 us -> 55.5 us (1.020)
  Pallas kernels: 53.6 us -> 54.7 us
    pallas_call x1, Pallas kernels: 51.5 us -> 52.6 us  [local(): pl.pallas_call(functools.partial(layer_kernel, n_row, n_col, heads), out_...]
where the time goes in v5:
time: 55.5 us; the launch traced here: 55.3 us
  Pallas kernels  54.7 us (99%)
  between operations  0.64 us (1%)
    pallas_call x1, Pallas kernels, local(): pl.pallas_call(functools.partial(layer_kernel, n_row, n_col, heads), out_...  52.6 us
    pallas_call x1, Pallas kernels, local(): pl.pallas_call(write_kernel, out_shape=tuple((jax.ShapeDtypeStruct(x.shap...  2.07 us

profile of v5, /device:TPU:0, one launch (start us, length us, event | category | flops | bytes accessed | tf_op | source)
XLA Modules:
  0.0 55.3 jit_solution(5006621592016683690)
XLA Ops:
  0.6 52.6 %layer.1 = (f32[64,192]{1,0:T(8,128)S(1)}, f32[64,128,128]{2,1,0:T(8,128)S(1)}, f32[16,128]{1,0:T(8,128)S(1)}) custom-call(f32[64,192]{1,0:T(8,128)} %single_hbm.1, f32[64,128,128]{2,1,0:T(8,128)} %pair_hbm.1, f32[768]{0:T(1024)} %gain_hbm.1, f32[1,128]{1,0:T(1,128)} %bitcast.6, f32[768,768]{1,0:T(8,128)} %wq_hbm.1, f32[768,768]{1,0:T(8,128)} %wk_hbm.1, ...), custom_call_target="tpu_custom_call" | custom-call | tf_op jit(solution)/shard_map/layer/pallas_call | solution.py:427
  53.3 2.1 %write_out.1 = (f32[64,192]{1,0:T(8,128)}, f32[64,128,128]{2,1,0:T(8,128)}, f32[16,128]{1,0:T(8,128)}) custom-call(f32[64,192]{1,0:T(8,128)S(1)} %get-tuple-element.9.refs_0_, f32[64,128,128]{2,1,0:T(8,128)S(1)} %get-tuple-element.10.refs_1_, f32[16,128]{1,0:T(8,128)S(1)} %get-tuple-element.11.refs_2_), custom_call_target="tpu_custom_call" | custom-call | tf_op jit(solution)/shard_map/write_out/pallas_call | solution.py:482
